TPU v7x, 32 devices: a whole 2x2x4 slice. The times are simulated.
32 devices in a mesh: fsdp: 16 (over z, x, core), tp: 2 (over y).
Axes of the slice: x: 2, y: 2, z: 4, core: 2. Of those that a mesh axis runs over, the one named last changes fastest.
Arguments:
- inputs: bfloat16 [32, 736, 1152], P('fsdp', 'tp'), may hold values from -6 to 6
- w_qkv: bfloat16 [3, 1152, 1152], P(None, 'fsdp', 'tp'), may hold values from -0.25 to 0.25
- w_out: bfloat16 [1152, 1152], P('tp', 'fsdp'), may hold values from -0.75 to 0.75
- w_up: bfloat16 [1152, 4304], P('fsdp', 'tp'), may hold values from -0.1875 to 0.1875
- w_down: bfloat16 [4304, 1152], P('tp', 'fsdp'), may hold values from -0.09375 to 0.09375
- norm_gains: float32 [2, 1152], replicated, may hold values from 0.1 to 1.9
- biases: float32 [6, 1152], replicated, may hold values from -3 to 3
- up_bias: float32 [4304], replicated, may hold values from -3 to 3
- cotangent: bfloat16 [32, 736, 1152], P('fsdp', 'tp'), may hold values from -6 to 6
Outputs:
- outputs: bfloat16 [32, 736, 1152], P('fsdp', 'tp')
- input_grad: float32 [32, 736, 1152], P('fsdp', 'tp')
- w_qkv_grad: float32 [3, 1152, 1152], P(None, 'fsdp', 'tp')
- w_out_grad: float32 [1152, 1152], P('tp', 'fsdp')
- w_up_grad: float32 [1152, 4304], P('fsdp', 'tp')
- w_down_grad: float32 [4304, 1152], P('tp', 'fsdp')
- norm_gains_grad: float32 [2, 1152], replicated
- biases_grad: float32 [6, 1152], replicated
- up_bias_grad: float32 [4304], replicated
All inputs are finite; a program needn't handle non-finite values.
Results may differ from a plain program's by a relative error of at most 0.018.
The roundings to bfloat16 on the way count: a program that leaves them out, or rounds other values in their place, can miss the bound.
Values may be sent and summed in bfloat16 or wider, within the bound.
A program may use at most 192 MiB of HBM per device.

v0:
```python
import math
import jax
import jax.numpy as jnp
from jax import lax
from jax.sharding import PartitionSpec as P

HD = 72
VALID = 729
norm_eps = 1e-06
gelu_coef = math.sqrt(2.0 / math.pi)


def norm_forward(values, scale_row, shift_row):
    average = jnp.mean(values, axis=-1, keepdims=True)
    centred = values - average
    inv_std = lax.rsqrt(jnp.mean(centred * centred, axis=-1, keepdims=True) + norm_eps)
    normed = centred * inv_std
    return (normed * scale_row + shift_row, normed, inv_std)


def norm_backward(upstream, normed, inv_std, scale_row):
    scaled = upstream * scale_row
    back = inv_std * (
        scaled
        - jnp.mean(scaled, axis=-1, keepdims=True)
        - normed * jnp.mean(scaled * normed, axis=-1, keepdims=True)
    )
    return (back, jnp.sum(upstream * normed, axis=0), jnp.sum(upstream, axis=0))


def gelu_tanh(pre_act):
    return (
        0.5
        * pre_act
        * (1.0 + jnp.tanh(gelu_coef * (pre_act + 0.044715 * pre_act * pre_act * pre_act)))
    )


def gelu_slope(pre_act):
    tangent = jnp.tanh(gelu_coef * (pre_act + 0.044715 * pre_act * pre_act * pre_act))
    inner_slope = gelu_coef * (1.0 + 3.0 * 0.044715 * pre_act * pre_act)
    return 0.5 * (1.0 + tangent) + 0.5 * pre_act * (1.0 - tangent * tangent) * inner_slope


def masked_scores(queries, key_rows, positions):
    seq_len = queries.shape[0]
    head_count = queries.shape[1] // HD
    query_heads = queries.reshape(seq_len, head_count, HD)
    key_heads = key_rows.reshape(seq_len, head_count, HD)
    scores = jnp.einsum("qhe,khe->hqk", query_heads, key_heads, preferred_element_type=jnp.float32)
    scores = scores * (1.0 / math.sqrt(HD))
    visible = (positions < VALID)[None, None, :]
    return (jnp.where(visible, scores, -1e30), query_heads, key_heads)


def attend_forward(queries, key_rows, values, positions):
    seq_len = queries.shape[0]
    scores, query_heads, key_heads = masked_scores(queries, key_rows, positions)
    value_heads = values.reshape(seq_len, -1, HD)
    largest = jnp.max(scores, axis=-1, keepdims=True)
    powers = jnp.exp(scores - largest)
    summed = jnp.sum(powers, axis=-1, keepdims=True)
    attn_probs = (powers / summed).astype(jnp.bfloat16)
    mixed_out = jnp.einsum(
        "hqk,khe->qhe", attn_probs, value_heads, preferred_element_type=jnp.float32
    )
    log_totals = (largest + jnp.log(summed))[:, :, 0]
    return (mixed_out.reshape(seq_len, queries.shape[1]).astype(jnp.bfloat16), log_totals)


def attend_backward(queries, key_rows, values, log_totals, d_mixed, positions):
    seq_len = queries.shape[0]
    scores, query_heads, key_heads = masked_scores(queries, key_rows, positions)
    value_heads = values.reshape(seq_len, -1, HD)
    grad_heads = d_mixed.reshape(seq_len, -1, HD)
    probs_full = jnp.exp(scores - log_totals[:, :, None])
    d_probs = jnp.einsum(
        "qhe,khe->hqk", grad_heads, value_heads, preferred_element_type=jnp.float32
    )
    row_inner = jnp.sum(probs_full * d_probs, axis=-1, keepdims=True)
    d_scores = (probs_full * (d_probs - row_inner)).astype(jnp.bfloat16)
    d_values = jnp.einsum(
        "hqk,qhe->khe",
        probs_full.astype(jnp.bfloat16),
        grad_heads,
        preferred_element_type=jnp.float32,
    )
    scale_now = 1.0 / math.sqrt(HD)
    d_queries = (
        jnp.einsum("hqk,khe->qhe", d_scores, key_heads, preferred_element_type=jnp.float32)
        * scale_now
    )
    d_keys = (
        jnp.einsum("hqk,qhe->khe", d_scores, query_heads, preferred_element_type=jnp.float32)
        * scale_now
    )
    parts = [d_queries, d_keys, d_values]
    return jnp.concatenate(
        [part.reshape(seq_len, queries.shape[1]).astype(jnp.bfloat16) for part in parts], axis=1
    )


def dot(left, right, dims):
    return lax.dot_general(left, right, (dims, ((), ())), preferred_element_type=jnp.float32)


ROWS_COLS = ((1,), (0,))
ROWS_ROWS = ((1,), (1,))
COLS_COLS = ((0,), (0,))


def swap_halves(block):
    return lax.ppermute(block, "tp", [(0, 1), (1, 0)])


def gather_rows(block):
    if lax.axis_size("tp") == 2:
        return jnp.concatenate([block, swap_halves(block)], axis=0)
    return lax.all_gather(block, "tp", axis=0, tiled=True)


def scatter_dot(left, right, dims):
    if lax.axis_size("tp") == 2:
        half = left.shape[0] // 2
        away = swap_halves(dot(left[half:], right, dims).astype(jnp.bfloat16))
        return dot(left[:half], right, dims) + away.astype(jnp.float32)
    return lax.psum_scatter(
        dot(left, right, dims).astype(jnp.bfloat16), "tp", scatter_dimension=0, tiled=True
    ).astype(jnp.float32)


def gather_weight(shard):
    return lax.all_gather(shard, "fsdp", axis=0, tiled=True)


def scatter_weight(whole):
    return lax.psum_scatter(
        whole.astype(jnp.bfloat16), "fsdp", scatter_dimension=0, tiled=False
    ).astype(jnp.float32)


def by_shard(whole):
    return whole.astype(jnp.bfloat16).reshape(lax.axis_size("fsdp"), -1, whole.shape[1])


def per_device(inputs, w_qkv, w_out, w_up, w_down, norm_gains, biases, up_bias, cotangent):
    image_count, rows_here, width = inputs.shape
    images = range(image_count)
    local_cols = w_qkv.shape[2]
    unit_count = w_up.shape[1]
    shard_rows = w_qkv.shape[1]
    tp_index = lax.axis_index("tp")
    seq_len = rows_here * lax.axis_size("tp")
    col_start = tp_index * local_cols
    unit_start = tp_index * unit_count
    positions = lax.iota(jnp.int32, seq_len)
    if lax.axis_size("tp") == 2:
        positions = positions + tp_index * rows_here
        positions = jnp.where(positions >= seq_len, positions - seq_len, positions)
    qkv_all = gather_weight(w_qkv.transpose(1, 0, 2).reshape(shard_rows, 3 * local_cols))
    out_all = gather_weight(w_out.T)
    up_all = gather_weight(w_up)
    down_all = gather_weight(w_down.T)
    query_bias = lax.dynamic_slice_in_dim(biases[1], col_start, local_cols)
    value_bias = lax.dynamic_slice_in_dim(biases[2], col_start, local_cols)
    unit_bias = lax.dynamic_slice_in_dim(up_bias, unit_start, unit_count)
    qkv_bias = jnp.concatenate([query_bias, jnp.zeros_like(query_bias), value_bias])
    residual = [inputs[i].astype(jnp.float32) for i in images]
    first = [norm_forward(residual[i], norm_gains[0], biases[0]) for i in images]
    gathered_one = [gather_rows(first[i][0].astype(jnp.bfloat16)) for i in images]
    grad_rows = [gather_rows(cotangent[i]) for i in images]
    saved, mixed, middle, second, gathered_two = ([], [], [], [], [])
    for i in images:
        projected = (dot(gathered_one[i], qkv_all, ROWS_COLS) + qkv_bias).astype(jnp.bfloat16)
        queries, key_rows, values = (
            projected[:, c * local_cols : (c + 1) * local_cols] for c in range(3)
        )
        mixed_out, log_totals = attend_forward(queries, key_rows, values, positions)
        saved.append((queries, key_rows, values, log_totals))
        mixed.append(mixed_out)
        middle.append(residual[i] + scatter_dot(mixed_out, out_all, ROWS_ROWS) + biases[3])
        second.append(norm_forward(middle[i], norm_gains[1], biases[4]))
        gathered_two.append(gather_rows(second[i][0].astype(jnp.bfloat16)))
    activated, d_pre, outputs, d_normed_two = ([], [], [], [])
    for i in images:
        pre_act = dot(gathered_two[i], up_all, ROWS_COLS) + unit_bias
        activated.append(gelu_tanh(pre_act).astype(jnp.bfloat16))
        d_act = dot(grad_rows[i], down_all, ROWS_COLS)
        d_pre.append((d_act * gelu_slope(pre_act)).astype(jnp.bfloat16))
        d_normed_two.append(scatter_dot(d_pre[i], up_all, ROWS_ROWS))
        mlp_rows = scatter_dot(activated[i], down_all, ROWS_ROWS)
        outputs.append((middle[i] + mlp_rows + biases[5]).astype(jnp.bfloat16))

    def joined(parts):
        return jnp.concatenate(parts, axis=0)

    grads_whole, units_whole = (joined(grad_rows), joined(d_pre))
    down_whole = by_shard(dot(grads_whole, joined(activated), COLS_COLS))
    up_whole = by_shard(dot(joined(gathered_two), units_whole, COLS_COLS))
    down_whole, up_whole, d_normed_two = lax.optimization_barrier(
        (down_whole, up_whole, d_normed_two)
    )
    down_grad = scatter_weight(down_whole).T
    up_grad = scatter_weight(up_whole)
    unit_sums = jnp.sum(units_whole, axis=0, dtype=jnp.float32)
    gain_two, shift_two, d_middle, branch = ([], [], [], [])
    for i in images:
        back, gain_part, shift_part = norm_backward(
            d_normed_two[i], second[i][1], second[i][2], norm_gains[1]
        )
        gain_two.append(gain_part)
        shift_two.append(shift_part)
        d_middle.append(cotangent[i].astype(jnp.float32) + back)
        branch.append(gather_rows(d_middle[i].astype(jnp.bfloat16)))
    d_qkv, d_normed_one = ([], [])
    for i in images:
        d_mixed = dot(branch[i], out_all, ROWS_COLS).astype(jnp.bfloat16)
        d_qkv.append(attend_backward(*saved[i], d_mixed, positions))
        d_normed_one.append(scatter_dot(d_qkv[i], qkv_all, ROWS_ROWS))
    out_grad = scatter_weight(by_shard(dot(joined(branch), joined(mixed), COLS_COLS))).T
    qkv_whole = joined(d_qkv)
    qkv_grad = scatter_weight(by_shard(dot(joined(gathered_one), qkv_whole, COLS_COLS)))
    qkv_grad = qkv_grad.reshape(shard_rows, 3, local_cols).transpose(1, 0, 2)
    qkv_sums = jnp.sum(qkv_whole, axis=0, dtype=jnp.float32)
    input_grad, gain_one, shift_one = ([], [], [])
    for i in images:
        back, gain_part, shift_part = norm_backward(
            d_normed_one[i], first[i][1], first[i][2], norm_gains[0]
        )
        gain_one.append(gain_part)
        shift_one.append(shift_part)
        input_grad.append(d_middle[i] + back)
    blank_row = jnp.zeros((width,), jnp.float32)
    query_sums = lax.dynamic_update_slice_in_dim(blank_row, qkv_sums[:local_cols], col_start, 0)
    value_sums = lax.dynamic_update_slice_in_dim(
        blank_row, qkv_sums[2 * local_cols :], col_start, 0
    )
    unit_row = lax.dynamic_update_slice_in_dim(jnp.zeros_like(up_bias), unit_sums, unit_start, 0)
    out_sums = sum((jnp.sum(d_middle[i], axis=0) for i in images))
    top_sums = jnp.sum(cotangent, axis=(0, 1), dtype=jnp.float32)
    pieces = [
        sum(gain_one),
        sum(shift_one),
        query_sums,
        value_sums,
        sum(gain_two),
        sum(shift_two),
        out_sums,
        top_sums,
        unit_row,
    ]
    total = lax.psum(jnp.concatenate(pieces), ("fsdp", "tp"))
    rows = total[: 8 * width].reshape(8, width)
    gain_total = jnp.stack([rows[0], rows[4]])
    bias_total = jnp.stack([rows[1], rows[2], rows[3], rows[6], rows[5], rows[7]])
    return (
        jnp.stack(outputs),
        jnp.stack(input_grad),
        qkv_grad,
        out_grad,
        up_grad,
        down_grad,
        gain_total,
        bias_total,
        total[8 * width :],
    )


def solution(mesh):
    return jax.shard_map(
        per_device,
        mesh=mesh,
        in_specs=(
            P("fsdp", "tp", None),
            P(None, "fsdp", "tp"),
            P("tp", "fsdp"),
            P("fsdp", "tp"),
            P("tp", "fsdp"),
            P(),
            P(),
            P(),
            P("fsdp", "tp", None),
        ),
        out_specs=(
            P("fsdp", "tp", None),
            P("fsdp", "tp", None),
            P(None, "fsdp", "tp"),
            P("tp", "fsdp"),
            P("fsdp", "tp"),
            P("tp", "fsdp"),
            P(),
            P(),
            P(),
        ),
        check_vma=False,
    )
```

profile of v0, /device:TPU:0, one launch (start us, length us, event | category | flops | bytes accessed | tf_op | source)
XLA Modules:
  0.0 743.1 jit_solution(5440039404475208873)
XLA Ops:
  16.4 3.0 collective-permute-start.4
  20.4 18.6 %collective-permute-done.4 = bf16[368,1152]{1,0:T(8,128)(2,1)S(1)} collective-permute-done((bf16[368,1152]{1,0:T(8,128)(2,1)S(1)}, bf16[368,1152]{1,0:T(8,128)(2,1)S(1)}, u32[]{:S(2)}, u32[]{:S(2)}) %collective-permute-start.4) | collective-permute-done | bytes 847904 | tf_op jit(solution)/shard_map/ppermute | solution.py:113
  39.0 24.9 %all-gather.5.cloned.1.call-done = bf16[1152,1728]{1,0:T(8,128)(2,1)} async-done(((bf16[72,1728]{1,0:T(8,128)(2,1)}), bf16[1152,1728]{1,0:T(8,128)(2,1)}) %all-gather.5.cloned.1.call-update) | async-done | bytes 3981328 | tf_op jit(solution)/shard_map/all_gather | solution.py:133
  63.9 6.5 add_convert_fusion
  75.1 2.6 copy.66
  77.7 6.3 add_convert_fusion.1
  84.1 2.0 fusion.199
  89.5 2.5 copy.62
  92.1 9.6 %fusion.204 = (f32[8,736]{1,0:T(8,128)}, f32[8,736,736]{1,2,0:T(8,128)}) fusion(bf16[736,8,72]{0,2,1:T(8,128)(2,1)S(1)} %bitcast.221, bf16[736,8,72]{0,2,1:T(8,128)(2,1)S(1)} %bitcast.211, pred[736]{0:T(1024)(128)(4,1)} %fusion.180), kind=kOutput, calls=%fused_computation.288 | convolution fusion | flops 637028608 | bytes 19054304 | tf_op jit(solution)/shard_map/qhe,khe->hqk/dot_general | solution.py:50
  101.7 9.4 %fusion = f32[8,736]{1,0:T(8,128)} fusion(f32[8,736,736]{1,2,0:T(8,128)} %get-tuple-element.110, f32[8,736]{1,0:T(8,128)} %get-tuple-element.109), kind=kLoop, calls=%fused_computation.12 | loop fusion | flops 8661248 | bytes 17381376 | tf_op jit(solution)/shard_map/reduce_sum | solution.py:62
  111.1 8.6 %fusion.157 = bf16[8,72,736]{2,1,0:T(8,128)(2,1)S(1)} fusion(bf16[736,8,72]{0,2,1:T(8,128)(2,1)S(1)} %bitcast.232, f32[8,736,736]{1,2,0:T(8,128)} %get-tuple-element.110, f32[8,736]{1,0:T(8,128)} %fusion, f32[8,736]{1,0:T(8,128)} %get-tuple-element.109), kind=kOutput, calls=%fused_computation.211 | convolution fusion | flops 637458432 | bytes 19077120 | tf_op jit(solution)/shard_map/hqk,khe->qhe/dot_general | solution.py:64
  120.8 3.2 convolution_convert_fusion.10
  125.5 9.2 %fusion.205 = (f32[8,736]{1,0:T(8,128)}, f32[8,736,736]{1,2,0:T(8,128)}) fusion(bf16[736,8,72]{0,2,1:T(8,128)(2,1)S(1)} %bitcast.223, bf16[736,8,72]{0,2,1:T(8,128)(2,1)S(1)} %bitcast.213, pred[736]{0:T(1024)(128)(4,1)S(1)} %copy-done.73), kind=kOutput, calls=%fused_computation.289 | convolution fusion | flops 637028608 | bytes 19054304 | tf_op jit(solution)/shard_map/qhe,khe->hqk/dot_general | solution.py:50
  134.7 8.8 %fusion.1 = f32[8,736]{1,0:T(8,128)S(1)} fusion(f32[8,736,736]{1,2,0:T(8,128)} %get-tuple-element.112, f32[8,736]{1,0:T(8,128)} %get-tuple-element.111), kind=kLoop, calls=%fused_computation.13 | loop fusion | flops 8661248 | bytes 17381376 | tf_op jit(solution)/shard_map/reduce_sum | solution.py:62
  143.5 8.8 %fusion.156 = bf16[8,72,736]{2,1,0:T(8,128)(2,1)S(1)} fusion(bf16[736,8,72]{0,2,1:T(8,128)(2,1)S(1)} %bitcast.234, f32[8,736,736]{1,2,0:T(8,128)} %get-tuple-element.112, f32[8,736]{1,0:T(8,128)S(1)} %fusion.1, f32[8,736]{1,0:T(8,128)S(1)} %copy-done.51), kind=kOutput, calls=%fused_computation.210 | convolution fusion | flops 637458432 | bytes 19077120 | tf_op jit(solution)/shard_map/hqk,khe->qhe/dot_general | solution.py:64
  154.8 19.7 %collective-permute-done.5 = bf16[368,1152]{1,0:T(8,128)(2,1)S(1)} collective-permute-done((bf16[368,1152]{1,0:T(8,128)(2,1)S(1)}, bf16[368,1152]{1,0:T(8,128)(2,1)S(1)}, u32[]{:S(2)}, u32[]{:S(2)}) %collective-permute-start.5) | collective-permute-done | bytes 847904 | tf_op jit(solution)/shard_map/ppermute | solution.py:113
  174.5 2.7 fusion.195
  185.2 16.6 %collective-permute-done.6 = bf16[368,1152]{1,0:T(8,128)(2,1)} collective-permute-done((bf16[368,1152]{1,0:T(8,128)(2,1)}, bf16[368,1152]{1,0:T(8,128)(2,1)}, u32[]{:S(2)}, u32[]{:S(2)}) %collective-permute-start.6) | collective-permute-done | bytes 847904 | tf_op jit(solution)/shard_map/ppermute | solution.py:113
  201.7 10.1 %fusion.112 = f32[736,2152]{1,0:T(8,128)} fusion(bf16[1152,2152]{1,0:T(8,128)(2,1)} %all-gather.9.cloned.1.call-done, bf16[368,1152]{1,0:T(8,128)(2,1)} %collective-permute-done.6, bf16[368,1152]{1,0:T(8,128)(2,1)} %get-tuple-element.102), kind=kOutput, calls=%fused_computation.155 | convolution fusion | flops 3652632576 | bytes 12989440 | tf_op jit(solution)/shard_map/dot_general | solution.py:104
  211.9 26.2 %collective-permute-done.9 = bf16[368,1152]{1,0:T(8,128)(2,1)} collective-permute-done((bf16[368,1152]{1,0:T(8,128)(2,1)}, bf16[368,1152]{1,0:T(8,128)(2,1)}, u32[]{:S(2)}, u32[]{:S(2)}) %collective-permute-start.9) | collective-permute-done | bytes 847904 | tf_op jit(solution)/shard_map/ppermute | solution.py:113
  238.1 11.2 %fusion.27 = bf16[736,2152]{1,0:T(8,128)(2,1)S(1)} fusion(bf16[1152,2152]{1,0:T(8,128)(2,1)} %all-gather.11.cloned.1.call-done, f32[736,2152]{1,0:T(8,128)} %fusion.112, f32[2152]{0:T(1024)S(1)} %dynamic_slice.17, bf16[368,1152]{1,0:T(8,128)(2,1)} %collective-permute-done.9, bf16[368,1152]{1,0:T(8,128)(2,1)} %get-tuple-element.86), kind=kOutput, calls=%fused_computation.46 | convolution fusion | flops 3684310016 | bytes 16165792 | tf_op jit(solution)/shard_map/dot_general | solution.py:104
  249.3 3.3 convolution_convert_fusion.5
  252.9 3.4 collective-permute-done.2
  256.2 11.5 %multiply_convert_fusion.3 = (bf16[736,2152]{1,0:T(8,128)(2,1)}, bf16[736,2152]{1,0:T(8,128)(2,1)}, f32[736,2152]{1,0:T(8,128)}) fusion(f32[2152]{0:T(1024)S(1)} %dynamic_slice.17, f32[736,2152]{1,0:T(8,128)} %fusion.112, bf16[1152,2152]{1,0:T(8,128)(2,1)S(1)} %copy-done.74, bf16[368,1152]{1,0:T(8,128)(2,1)} %collective-permute-done.2, ...), kind=kOutput, calls=%fused_computation.52 | convolution fusion | flops 3684310016 | bytes 25669024 | tf_op jit(solution)/shard_map/dot_general | solution.py:104
  267.7 9.5 %fusion.21 = bf16[736,2152]{1,0:T(8,128)(2,1)S(1)} fusion(bf16[1152,2152]{1,0:T(8,128)(2,1)S(1)} %bitcast.253, f32[736,2152]{1,0:T(8,128)} %get-tuple-element.113, f32[2152]{0:T(1024)S(1)} %dynamic_slice.17, bf16[368,1152]{1,0:T(8,128)(2,1)} %collective-permute-done.8, bf16[368,1152]{1,0:T(8,128)(2,1)} %get-tuple-element.85), kind=kOutput, calls=%fused_computation.40 | convolution fusion | flops 3684310016 | bytes 16165792 | tf_op jit(solution)/shard_map/dot_general | solution.py:104
  277.3 3.3 convolution_convert_fusion.6
  280.8 14.3 %convolution_convert_fusion = bf16[1152,2152]{0,1:T(8,128)(2,1)} fusion(bf16[736,2152]{1,0:T(8,128)(2,1)S(1)} %fusion.27, bf16[736,2152]{1,0:T(8,128)(2,1)S(1)} %fusion.21, bf16[368,1152]{1,0:T(8,128)(2,1)} %collective-permute-done.6, bf16[368,1152]{1,0:T(8,128)(2,1)} %get-tuple-element.102, bf16[368,1152]{1,0:T(8,128)(2,1)} %collective-permute-done.2, ...), kind=kOutput, calls=%fused_computation.17 | convolution fusion | flops 7327198208 | bytes 14685184 | tf_op jit(solution)/shard_map/dot_general | solution.py:104
  295.1 14.0 %convolution_convert_fusion.1 = bf16[1152,2152]{0,1:T(8,128)(2,1)} fusion(bf16[736,2152]{1,0:T(8,128)(2,1)S(1)} %copy-done.83, bf16[736,2152]{1,0:T(8,128)(2,1)S(1)} %copy-done.80, bf16[368,1152]{1,0:T(8,128)(2,1)} %collective-permute-done.9, bf16[368,1152]{1,0:T(8,128)(2,1)} %get-tuple-element.86, bf16[368,1152]{1,0:T(8,128)(2,1)} %collective-permute-done.8, ...), kind=kOutput, calls=%fused_computation.18 | convolution fusion | flops 7327198208 | bytes 14685184 | tf_op jit(solution)/shard_map/dot_general | solution.py:104
  309.1 8.4 %copy.71 = bf16[1152,2152]{1,0:T(8,128)(2,1)} copy(bf16[1152,2152]{0,1:T(8,128)(2,1)} %convolution_convert_fusion) | data formatting | bytes 9916416 | tf_op jit(solution)/shard_map/convert_element_type | solution.py:143
  317.5 8.8 %copy.70 = bf16[1152,2152]{1,0:T(8,128)(2,1)} copy(bf16[1152,2152]{0,1:T(8,128)(2,1)} %convolution_convert_fusion.1) | data formatting | bytes 9916416 | tf_op jit(solution)/shard_map/convert_element_type | solution.py:143
  326.3 6.9 convert_add_fusion.2
  333.1 6.2 convert_add_fusion.3
  339.4 4.1 multiply_reduce_fusion.3
  343.5 2.1 fusion.194
  348.0 19.6 %collective-permute-done.14 = bf16[368,1152]{1,0:T(8,128)(2,1)S(1)} collective-permute-done((bf16[368,1152]{1,0:T(8,128)(2,1)S(1)}, bf16[368,1152]{1,0:T(8,128)(2,1)S(1)}, u32[]{:S(2)}, u32[]{:S(2)}) %collective-permute-start.14) | collective-permute-done | bytes 847904 | tf_op jit(solution)/shard_map/ppermute | solution.py:113
  369.0 11.6 %multiply_reduce_fusion = (f32[8,736]{1,0:T(8,128)S(1)}, f32[8,736,736]{1,2,0:T(8,128)}) fusion(f32[8,736,736]{1,2,0:T(8,128)} %get-tuple-element.112, f32[8,736]{1,0:T(8,128)S(1)} %log_add_fusion, bf16[736,8,72]{0,2,1:T(8,128)(2,1)S(1)} %bitcast.236, bf16[736,8,72]{0,2,1:T(8,128)(2,1)S(1)} %bitcast.235), kind=kOutput, calls=%fused_computation.1 | convolution fusion | flops 637028608 | bytes 36411392 | tf_op jit(solution)/shard_map/qhe,khe->hqk/dot_general | solution.py:77
  380.6 12.7 %multiply_convert_fusion = bf16[8,736,736]{1,2,0:T(8,128)(2,1)S(1)} fusion(f32[8,736,736]{1,2,0:T(8,128)} %get-tuple-element.117, f32[8,736,736]{1,2,0:T(8,128)} %get-tuple-element.112, f32[8,736]{1,0:T(8,128)S(1)} %get-tuple-element.116, f32[8,736]{1,0:T(8,128)S(1)} %log_add_fusion), kind=kLoop, calls=%fused_computation | loop fusion | flops 17334272 | bytes 43382784 | tf_op jit(solution)/shard_map/convert_element_type | solution.py:81
  393.3 3.7 multiply_convert_fusion.4
  397.0 2.6 multiply_convert_fusion.5
  399.6 9.9 %fusion.161 = bf16[8,72,736]{2,1,0:T(8,128)(2,1)} fusion(bf16[736,8,72]{0,2,1:T(8,128)(2,1)S(1)} %bitcast.237, f32[8,736,736]{1,2,0:T(8,128)} %get-tuple-element.112, f32[8,736]{1,0:T(8,128)S(1)} %log_add_fusion), kind=kOutput, calls=%fused_computation.213 | convolution fusion | flops 633124864 | bytes 19053568 | tf_op jit(solution)/shard_map/hqk,qhe->khe/dot_general | solution.py:82
  410.9 9.9 %fusion.158 = bf16[8,72,736]{2,1,0:T(8,128)(2,1)} fusion(bf16[736,8,72]{0,2,1:T(8,128)(2,1)S(1)} %bitcast.238, f32[8,736,736]{1,2,0:T(8,128)} %get-tuple-element.110, f32[8,736]{1,0:T(8,128)S(1)} %log_add_fusion.1), kind=kOutput, calls=%fused_computation.212 | convolution fusion | flops 633124864 | bytes 19053568 | tf_op jit(solution)/shard_map/hqk,qhe->khe/dot_general | solution.py:82
  420.9 12.0 %multiply_reduce_fusion.1 = (f32[8,736]{1,0:T(8,128)S(1)}, f32[8,736,736]{1,2,0:T(8,128)}) fusion(f32[8,736,736]{1,2,0:T(8,128)} %get-tuple-element.110, f32[8,736]{1,0:T(8,128)S(1)} %log_add_fusion.1, bf16[736,8,72]{0,2,1:T(8,128)(2,1)S(1)} %bitcast.239, bf16[736,8,72]{0,2,1:T(8,128)(2,1)S(1)} %bitcast.233), kind=kOutput, calls=%fused_computation.4 | convolution fusion | flops 637028608 | bytes 36411392 | tf_op jit(solution)/shard_map/qhe,khe->hqk/dot_general | solution.py:77
  432.9 3.6 fusion.60
  436.5 2.6 copy.79
  439.2 13.1 %multiply_convert_fusion.1 = bf16[8,736,736]{1,2,0:T(8,128)(2,1)S(1)} fusion(f32[8,736,736]{1,2,0:T(8,128)} %get-tuple-element.115, f32[8,736,736]{1,2,0:T(8,128)} %get-tuple-element.110, f32[8,736]{1,0:T(8,128)S(1)} %get-tuple-element.114, f32[8,736]{1,0:T(8,128)S(1)} %log_add_fusion.1), kind=kLoop, calls=%fused_computation.3 | loop fusion | flops 17334272 | bytes 43382784 | tf_op jit(solution)/shard_map/convert_element_type | solution.py:81
  452.3 2.8 multiply_convert_fusion.6
  458.5 10.3 %convolution_convert_fusion.2 = bf16[1152,1728]{0,1:T(8,128)(2,1)} fusion(bf16[368,1152]{1,0:T(8,128)(2,1)S(1)} %copy-done.77, bf16[368,1152]{1,0:T(8,128)(2,1)S(1)} %copy-done.49, bf16[368,1152]{1,0:T(8,128)(2,1)S(1)} %copy-done.79, bf16[368,1152]{1,0:T(8,128)(2,1)} %get-tuple-element.77, bf16[736,576]{0,1:T(8,128)(2,1)S(1)} %bitcast.225, ...), kind=kOutput, calls=%fused_computation.30 | convolution fusion | flops 5906571264 | bytes 12460032 | tf_op jit(solution)/shard_map/dot_general | solution.py:104
  468.8 6.4 copy.78
  478.0 6.3 convolution_convert_fusion.7
  485.8 6.1 convolution_convert_fusion.9
  493.8 11.8 %collective-permute-done.7 = bf16[368,1152]{1,0:T(8,128)(2,1)} collective-permute-done((bf16[368,1152]{1,0:T(8,128)(2,1)}, bf16[368,1152]{1,0:T(8,128)(2,1)}, u32[]{:S(2)}, u32[]{:S(2)}) %collective-permute-start.7) | collective-permute-done | bytes 847904 | tf_op jit(solution)/shard_map/ppermute | solution.py:113
  505.7 6.2 fusion.145
  511.8 2.9 collective-permute-done.3
  514.7 5.3 fusion.153
  526.3 2.5 convolution_convert_fusion.3
  530.6 2.5 convolution_convert_fusion.4
  533.4 23.4 %convert_reduce_fusion.1 = f32[1728]{0:T(1024)S(1)} fusion(bf16[736,576]{0,1:T(8,128)(2,1)S(1)} %bitcast.227, bf16[736,576]{0,1:T(8,128)(2,1)S(1)} %bitcast.217, bf16[736,576]{0,1:T(8,128)(2,1)S(1)} %bitcast.207, bf16[736,576]{0,1:T(8,128)(2,1)S(1)} %bitcast.230, bf16[736,576]{0,1:T(8,128)(2,1)S(1)} %bitcast.220, bf16[736,576]{0,1:T(8,128)(2,1)S(1)} %bitcast.210), kind=kLoop, calls=%fused_computation.19 | loop fusion | flops 33065280 | bytes 5094144 | tf_op jit(solution)/shard_map/reduce_sum | solution.py:224
  557.3 2.0 convert_add_fusion
  559.5 4.3 fusion.98
  564.0 39.7 %psum.7 = f32[13520]{0:T(1024)S(1)} all-reduce(f32[13520]{0:T(1024)S(1)} %constant_dynamic-update-slice_fusion), channel_id=1, replica_groups=mesh['fsdp'=16,'tp'=2] {'fsdp','tp'}, use_global_device_ids=true, to_apply=%region_39.40 | all-reduce | flops 13520 | bytes 108160 | tf_op jit(solution)/shard_map/psum | solution.py:252
  605.7 3.1 fusion.97
  608.8 2.0 pad_maximum_fusion.2
  614.4 38.4 %reduce-scatter.17.cloned.1.call-done = bf16[1,72,2152]{2,1,0:T(8,128)(2,1)} async-done(((bf16[16,72,2152]{2,1,0:T(8,128)(2,1)}), bf16[1,72,2152]{2,1,0:T(8,128)(2,1)}) %reduce-scatter.17.cloned.1.call-update) | async-done | bytes 309904
  654.6 79.5 %reduce-scatter.15.cloned.1.call-done = bf16[1,72,2152]{2,1,0:T(8,128)(2,1)} async-done(((bf16[16,72,2152]{2,1,0:T(8,128)(2,1)}), bf16[1,72,2152]{2,1,0:T(8,128)(2,1)}) %reduce-scatter.15.cloned.1.call-update) | async-done | bytes 309904
  (302 shorter events, 64.6 us)
Async XLA Ops:
  7.2 7.0 copy-start.66
  7.2 56.7 %all-gather.5.cloned.1.call-start = ((), (), s32[]{:S(2)}) async-start(), calls=%async_computation.4 | async-start | bytes 4386816 | tf_op jit(solution)/shard_map/all_gather | solution.py:133
  9.4 111.3 %all-gather.7.cloned.1.call-start = ((), (), s32[]{:S(2)}) async-start(), calls=%async_computation.5 | async-start | bytes 1566720 | tf_op jit(solution)/shard_map/all_gather | solution.py:133
  10.2 191.6 %all-gather.9.cloned.1.call-start = ((), (), s32[]{:S(2)}) async-start(), calls=%async_computation.6 | async-start | bytes 5326848 | tf_op jit(solution)/shard_map/all_gather | solution.py:133
  10.9 227.2 %all-gather.11.cloned.1.call-start = ((), (), s32[]{:S(2)}) async-start(), calls=%async_computation.7 | async-start | bytes 5326848 | tf_op jit(solution)/shard_map/all_gather | solution.py:133
  13.5 50.4 %copy-start.59 = (f32[368]{0:T(512)}, f32[368]{0:T(512)S(1)}, u32[]{:S(2)}) copy-start(f32[368]{0:T(512)S(1)} %get-tuple-element.121) | copy-start | bytes 4420
  13.5 50.4 %copy-start.61 = (f32[368]{0:T(512)}, f32[368]{0:T(512)S(1)}, u32[]{:S(2)}) copy-start(f32[368]{0:T(512)S(1)} %get-tuple-element.122) | copy-start | bytes 4420
  14.1 49.8 %copy-start.67 = (f32[368]{0:T(512)}, f32[368]{0:T(512)S(1)}, u32[]{:S(2)}) copy-start(f32[368]{0:T(512)S(1)} %add_rsqrt_fusion.3) | copy-start | bytes 4420
  14.2 49.7 %copy-start.69 = (f32[368]{0:T(512)}, f32[368]{0:T(512)S(1)}, u32[]{:S(2)}) copy-start(f32[368]{0:T(512)S(1)} %add_rsqrt_fusion.1) | copy-start | bytes 4420
  16.4 47.5 %copy-start.48 = (bf16[368,1152]{1,0:T(8,128)(2,1)}, bf16[368,1152]{1,0:T(8,128)(2,1)S(1)}, u32[]{:S(2)}) copy-start(bf16[368,1152]{1,0:T(8,128)(2,1)S(1)} %get-tuple-element.78) | copy-start | bytes 2543620
  16.4 22.7 %collective-permute-start.4 = (bf16[368,1152]{1,0:T(8,128)(2,1)S(1)}, bf16[368,1152]{1,0:T(8,128)(2,1)S(1)}, u32[]{:S(2)}, u32[]{:S(2)}) collective-permute-start(bf16[368,1152]{1,0:T(8,128)(2,1)S(1)} %get-tuple-element.78), channel_id=1, source_target_pairs={{0,1},{1,0},{2,3},{3,2},{4,5},{5,4},{6,7},{7,6},{8,9},{9,8},{10,11... | collective-permute-start | bytes 2543624 | tf_op jit(solution)/shard_map/ppermute | solution.py:113
  19.4 58.4 %collective-permute-start = (bf16[368,1152]{1,0:T(8,128)(2,1)}, bf16[368,1152]{1,0:T(8,128)(2,1)S(1)}, u32[]{:S(2)}, u32[]{:S(2)}) collective-permute-start(bf16[368,1152]{1,0:T(8,128)(2,1)} %get-tuple-element.77), channel_id=1, source_target_pairs={{0,1},{1,0},{2,3},{3,2},{4,5},{5,4},{6,7},{7,6},{8,9},{9,8},{10,11... | collective-permute-start | bytes 2543624 | tf_op jit(solution)/shard_map/ppermute | solution.py:113
  19.4 591.3 %reduce-scatter.13.cloned.1.call-start = ((), (), s32[]{:S(2)}) async-start(), calls=%async_computation.9 | async-start | bytes 1566720
  39.0 24.9 %copy-start.76 = (bf16[368,1152]{1,0:T(8,128)(2,1)}, bf16[368,1152]{1,0:T(8,128)(2,1)S(1)}, u32[]{:S(2)}) copy-start(bf16[368,1152]{1,0:T(8,128)(2,1)S(1)} %collective-permute-done.4) | copy-start | bytes 2543620
  73.3 52.2 %copy-start.14 = (bf16[736,576]{0,1:T(8,128)(2,1)}, bf16[736,576]{0,1:T(8,128)(2,1)S(1)}, u32[]{:S(2)}) copy-start(bf16[736,576]{0,1:T(8,128)(2,1)S(1)} %copy.68) | copy-start | bytes 2543620
  75.1 50.3 %copy-start.22 = (bf16[736,576]{0,1:T(8,128)(2,1)}, bf16[736,576]{0,1:T(8,128)(2,1)S(1)}, u32[]{:S(2)}) copy-start(bf16[736,576]{0,1:T(8,128)(2,1)S(1)} %copy.67) | copy-start | bytes 2543620
  87.6 14.1 %copy-start.12 = (bf16[736,576]{0,1:T(8,128)(2,1)}, bf16[736,576]{0,1:T(8,128)(2,1)S(1)}, u32[]{:S(2)}) copy-start(bf16[736,576]{0,1:T(8,128)(2,1)S(1)} %copy.64) | copy-start | bytes 2543620
  89.5 12.2 %copy-start.20 = (bf16[736,576]{0,1:T(8,128)(2,1)}, bf16[736,576]{0,1:T(8,128)(2,1)S(1)}, u32[]{:S(2)}) copy-start(bf16[736,576]{0,1:T(8,128)(2,1)S(1)} %copy.63) | copy-start | bytes 2543620
  101.7 9.4 %copy-start.32 = (bf16[736,576]{0,1:T(8,128)(2,1)S(1)}, bf16[736,576]{0,1:T(8,128)(2,1)}, u32[]{:S(2)}) copy-start(bf16[736,576]{0,1:T(8,128)(2,1)} %copy.62) | copy-start | bytes 2543620
  119.7 15.0 %copy-start.43 = (bf16[8,72,736]{2,1,0:T(8,128)(2,1)}, bf16[8,72,736]{2,1,0:T(8,128)(2,1)S(1)}, u32[]{:S(2)}) copy-start(bf16[8,72,736]{2,1,0:T(8,128)(2,1)S(1)} %fusion.157) | copy-start | bytes 2543620
  124.0 30.8 %collective-permute-start.1 = (bf16[368,1152]{1,0:T(8,128)(2,1)}, bf16[368,1152]{1,0:T(8,128)(2,1)}, u32[]{:S(2)}, u32[]{:S(2)}) collective-permute-start(bf16[368,1152]{1,0:T(8,128)(2,1)} %convolution_convert_fusion.10), channel_id=1, source_target_pairs={{0,1},{1,0},{2,3},{3,2},{4,5},{5,4},{6,7},{7,6},{8,9},{9,8},{10,11... | collective-permute-start | bytes 2543624 | tf_op jit(solution)/shard_map/ppermute | solution.py:113
  134.7 8.8 %copy-start.34 = (bf16[736,576]{0,1:T(8,128)(2,1)S(1)}, bf16[736,576]{0,1:T(8,128)(2,1)}, u32[]{:S(2)}) copy-start(bf16[736,576]{0,1:T(8,128)(2,1)} %copy.66) | copy-start | bytes 2543620
  134.7 8.8 %copy-start.51 = (f32[8,736]{1,0:T(8,128)S(1)}, f32[8,736]{1,0:T(8,128)}, u32[]{:S(2)}) copy-start(f32[8,736]{1,0:T(8,128)} %get-tuple-element.111) | copy-start | bytes 70660
  143.5 9.1 %copy-start.30 = (bf16[1152,576]{1,0:T(8,128)(2,1)S(1)}, bf16[1152,576]{1,0:T(8,128)(2,1)}, u32[]{:S(2)}) copy-start(bf16[1152,576]{1,0:T(8,128)(2,1)} %all-gather.7.cloned.1.call-done) | copy-start | bytes 3981316
  152.5 21.9 %copy-start.1 = (bf16[2,368,1152]{2,1,0:T(8,128)(2,1)S(1)}, bf16[2,368,1152]{2,1,0:T(8,128)(2,1)}, u32[]{:S(2)}) copy-start(bf16[2,368,1152]{2,1,0:T(8,128)(2,1)} %param.9) | copy-start | bytes 5087236
  152.6 21.9 %copy-start.41 = (bf16[368,8,72]{0,2,1:T(8,128)(2,1)S(1)}, bf16[368,8,72]{0,2,1:T(8,128)(2,1)}, u32[]{:S(2)}) copy-start(bf16[368,8,72]{0,2,1:T(8,128)(2,1)} %get-tuple-element.88) | copy-start | bytes 1271812
  152.6 21.9 %copy-start.65 = (f32[1152]{0:T(1024)S(1)}, f32[1152]{0:T(1024)}, u32[]{:S(2)}) copy-start(f32[1152]{0:T(1024)} %get-tuple-element.58) | copy-start | bytes 13828
  153.6 20.9 %collective-permute-start.5 = (bf16[368,1152]{1,0:T(8,128)(2,1)S(1)}, bf16[368,1152]{1,0:T(8,128)(2,1)S(1)}, u32[]{:S(2)}, u32[]{:S(2)}) collective-permute-start(bf16[368,1152]{1,0:T(8,128)(2,1)S(1)} %convolution_convert_fusion.8), channel_id=1, source_target_pairs={{0,1},{1,0},{2,3},{3,2},{4,5},{5,4},{6,7},{7,6},{8,9},{9,8},{10,11... | collective-permute-start | bytes 2543624 | tf_op jit(solution)/shard_map/ppermute | solution.py:113
  179.6 22.1 %collective-permute-start.6 = (bf16[368,1152]{1,0:T(8,128)(2,1)}, bf16[368,1152]{1,0:T(8,128)(2,1)}, u32[]{:S(2)}, u32[]{:S(2)}) collective-permute-start(bf16[368,1152]{1,0:T(8,128)(2,1)} %get-tuple-element.102), channel_id=1, source_target_pairs={{0,1},{1,0},{2,3},{3,2},{4,5},{5,4},{6,7},{7,6},{8,9},{9,8},{10,11... | collective-permute-start | bytes 2543624 | tf_op jit(solution)/shard_map/ppermute | solution.py:113
  181.3 86.4 %collective-permute-start.8 = (bf16[368,1152]{1,0:T(8,128)(2,1)}, bf16[368,1152]{1,0:T(8,128)(2,1)}, u32[]{:S(2)}, u32[]{:S(2)}) collective-permute-start(bf16[368,1152]{1,0:T(8,128)(2,1)} %get-tuple-element.85), channel_id=1, source_target_pairs={{0,1},{1,0},{2,3},{3,2},{4,5},{5,4},{6,7},{7,6},{8,9},{9,8},{10,11... | collective-permute-start | bytes 2543624 | tf_op jit(solution)/shard_map/ppermute | solution.py:113
  183.0 55.0 %collective-permute-start.9 = (bf16[368,1152]{1,0:T(8,128)(2,1)}, bf16[368,1152]{1,0:T(8,128)(2,1)}, u32[]{:S(2)}, u32[]{:S(2)}) collective-permute-start(bf16[368,1152]{1,0:T(8,128)(2,1)} %get-tuple-element.86), channel_id=1, source_target_pairs={{0,1},{1,0},{2,3},{3,2},{4,5},{5,4},{6,7},{7,6},{8,9},{9,8},{10,11... | collective-permute-start | bytes 2543624 | tf_op jit(solution)/shard_map/ppermute | solution.py:113
  183.4 72.8 %collective-permute-start.2 = (bf16[368,1152]{1,0:T(8,128)(2,1)}, bf16[368,1152]{1,0:T(8,128)(2,1)}, u32[]{:S(2)}, u32[]{:S(2)}) collective-permute-start(bf16[368,1152]{1,0:T(8,128)(2,1)} %get-tuple-element.101), channel_id=1, source_target_pairs={{0,1},{1,0},{2,3},{3,2},{4,5},{5,4},{6,7},{7,6},{8,9},{9,8},{10,11... | collective-permute-start | bytes 2543624 | tf_op jit(solution)/shard_map/ppermute | solution.py:113
  238.1 11.2 %copy-start.74 = (bf16[1152,2152]{1,0:T(8,128)(2,1)S(1)}, bf16[1152,2152]{1,0:T(8,128)(2,1)}, u32[]{:S(2)}) copy-start(bf16[1152,2152]{1,0:T(8,128)(2,1)} %all-gather.9.cloned.1.call-done) | copy-start | bytes 14874628
  249.3 31.5 %copy-start.36 = (bf16[736,2152]{1,0:T(8,128)(2,1)}, bf16[736,2152]{1,0:T(8,128)(2,1)S(1)}, u32[]{:S(2)}) copy-start(bf16[736,2152]{1,0:T(8,128)(2,1)S(1)} %fusion.27) | copy-start | bytes 9503236
  249.3 18.4 %slice-start = ((s8[5013504]{0:T(1024)(128)(4,1)}), s8[4194304]{0:T(1024)(128)(4,1)S(1)}, s32[]{:S(2)}) async-start(s8[5013504]{0:T(1024)(128)(4,1)} %bitcast.252), calls=%async_computation.12 | async-start | bytes 8388608
  252.6 15.1 %slice-start.1 = ((s8[5013504]{0:T(1024)(128)(4,1)}), s8[819200]{0:T(1024)(128)(4,1)S(1)}, s32[]{:S(2)}) async-start(s8[5013504]{0:T(1024)(128)(4,1)} %bitcast.252), calls=%async_computation.13 | async-start | bytes 1638400
  252.6 73.7 %collective-permute-start.11 = (bf16[368,1152]{1,0:T(8,128)(2,1)}, bf16[368,1152]{1,0:T(8,128)(2,1)}, u32[]{:S(2)}, u32[]{:S(2)}) collective-permute-start(bf16[368,1152]{1,0:T(8,128)(2,1)} %convolution_convert_fusion.5), channel_id=1, source_target_pairs={{0,1},{1,0},{2,3},{3,2},{4,5},{5,4},{6,7},{7,6},{8,9},{9,8},{10,11... | collective-permute-start | bytes 2543624 | tf_op jit(solution)/shard_map/ppermute | solution.py:113
  280.5 14.6 %copy-start.80 = (bf16[736,2152]{1,0:T(8,128)(2,1)S(1)}, bf16[736,2152]{1,0:T(8,128)(2,1)}, u32[]{:S(2)}) copy-start(bf16[736,2152]{1,0:T(8,128)(2,1)} %get-tuple-element.103) | copy-start | bytes 9503236
  280.5 14.6 %copy-start.83 = (bf16[736,2152]{1,0:T(8,128)(2,1)S(1)}, bf16[736,2152]{1,0:T(8,128)(2,1)}, u32[]{:S(2)}) copy-start(bf16[736,2152]{1,0:T(8,128)(2,1)} %get-tuple-element.104) | copy-start | bytes 9503236
  280.5 52.6 %collective-permute-start.10 = (bf16[368,1152]{1,0:T(8,128)(2,1)}, bf16[368,1152]{1,0:T(8,128)(2,1)}, u32[]{:S(2)}, u32[]{:S(2)}) collective-permute-start(bf16[368,1152]{1,0:T(8,128)(2,1)} %convolution_convert_fusion.6), channel_id=1, source_target_pairs={{0,1},{1,0},{2,3},{3,2},{4,5},{5,4},{6,7},{7,6},{8,9},{9,8},{10,11... | collective-permute-start | bytes 2543624 | tf_op jit(solution)/shard_map/ppermute | solution.py:113
  345.6 23.4 %copy-start.5 = (f32[368,1152]{1,0:T(8,128)}, f32[368,1152]{1,0:T(8,128)S(1)}, u32[]{:S(2)}) copy-start(f32[368,1152]{1,0:T(8,128)S(1)} %get-tuple-element.66) | copy-start | bytes 5087236
  345.6 23.4 %copy-start.7 = (f32[368,1152]{1,0:T(8,128)}, f32[368,1152]{1,0:T(8,128)S(1)}, u32[]{:S(2)}) copy-start(f32[368,1152]{1,0:T(8,128)S(1)} %get-tuple-element.82) | copy-start | bytes 5087236
  345.6 22.0 %copy-start.31 = (bf16[1152,576]{1,0:T(8,128)(2,1)S(1)}, bf16[1152,576]{1,0:T(8,128)(2,1)}, u32[]{:S(2)}) copy-start(bf16[1152,576]{1,0:T(8,128)(2,1)} %all-gather.7.cloned.1.call-done) | copy-start | bytes 3981316
  345.7 21.9 %collective-permute-start.14 = (bf16[368,1152]{1,0:T(8,128)(2,1)S(1)}, bf16[368,1152]{1,0:T(8,128)(2,1)S(1)}, u32[]{:S(2)}, u32[]{:S(2)}) collective-permute-start(bf16[368,1152]{1,0:T(8,128)(2,1)S(1)} %convert_element_type.297), channel_id=1, source_target_pairs={{0,1},{1,0},{2,3},{3,2},{4,5},{5,4},{6,7},{7,6},{8,9},{9,8},{10,11... | collective-permute-start | bytes 2543624 | tf_op jit(solution)/shard_map/ppermute | solution.py:113
  347.4 21.6 %copy-start.35 = (bf16[736,576]{0,1:T(8,128)(2,1)S(1)}, bf16[736,576]{0,1:T(8,128)(2,1)}, u32[]{:S(2)}) copy-start(bf16[736,576]{0,1:T(8,128)(2,1)} %copy.66) | copy-start | bytes 2543620
  347.4 62.1 %collective-permute-start.12 = (bf16[368,1152]{1,0:T(8,128)(2,1)S(1)}, bf16[368,1152]{1,0:T(8,128)(2,1)S(1)}, u32[]{:S(2)}, u32[]{:S(2)}) collective-permute-start(bf16[368,1152]{1,0:T(8,128)(2,1)S(1)} %convert_element_type.281), channel_id=1, source_target_pairs={{0,1},{1,0},{2,3},{3,2},{4,5},{5,4},{6,7},{7,6},{8,9},{9,8},{10,11... | collective-permute-start | bytes 2543624 | tf_op jit(solution)/shard_map/ppermute | solution.py:113
  380.6 12.7 %copy-start.23 = (bf16[736,576]{0,1:T(8,128)(2,1)S(1)}, bf16[736,576]{0,1:T(8,128)(2,1)}, u32[]{:S(2)}) copy-start(bf16[736,576]{0,1:T(8,128)(2,1)} %copy-done.22) | copy-start | bytes 2543620
  410.9 10.0 %copy-start.33 = (bf16[736,576]{0,1:T(8,128)(2,1)S(1)}, bf16[736,576]{0,1:T(8,128)(2,1)}, u32[]{:S(2)}) copy-start(bf16[736,576]{0,1:T(8,128)(2,1)} %copy.62) | copy-start | bytes 2543620
  420.9 12.0 %copy-start.44 = (bf16[8,72,736]{2,1,0:T(8,128)(2,1)S(1)}, bf16[8,72,736]{2,1,0:T(8,128)(2,1)}, u32[]{:S(2)}) copy-start(bf16[8,72,736]{2,1,0:T(8,128)(2,1)} %copy-done.43) | copy-start | bytes 2543620
  420.9 12.0 %copy-start.46 = (bf16[8,72,736]{2,1,0:T(8,128)(2,1)S(1)}, bf16[8,72,736]{2,1,0:T(8,128)(2,1)}, u32[]{:S(2)}) copy-start(bf16[8,72,736]{2,1,0:T(8,128)(2,1)} %copy-done.45) | copy-start | bytes 2543620
  439.2 173.1 %reduce-scatter.11.cloned.1.call-start = ((), (), s32[]{:S(2)}) async-start(), calls=%async_computation.8 | async-start | bytes 4386816 | tf_op jit(solution)/shard_map/reduce_scatter | solution.py:137
  439.2 13.1 %copy-start.21 = (bf16[736,576]{0,1:T(8,128)(2,1)S(1)}, bf16[736,576]{0,1:T(8,128)(2,1)}, u32[]{:S(2)}) copy-start(bf16[736,576]{0,1:T(8,128)(2,1)} %copy-done.20) | copy-start | bytes 2543620
  475.3 177.5 %reduce-scatter.17.cloned.1.call-start = ((), (), s32[]{:S(2)}) async-start(), calls=%async_computation.11 | async-start | bytes 5326848
  476.0 258.2 %reduce-scatter.15.cloned.1.call-start = ((), (), s32[]{:S(2)}) async-start(), calls=%async_computation.10 | async-start | bytes 5326848
  478.0 7.8 %copy-start.81 = (bf16[736,2152]{1,0:T(8,128)(2,1)S(1)}, bf16[736,2152]{1,0:T(8,128)(2,1)}, u32[]{:S(2)}) copy-start(bf16[736,2152]{1,0:T(8,128)(2,1)} %get-tuple-element.103) | copy-start | bytes 9503236
  484.4 8.1 %copy-start.37 = (bf16[736,2152]{1,0:T(8,128)(2,1)S(1)}, bf16[736,2152]{1,0:T(8,128)(2,1)}, u32[]{:S(2)}) copy-start(bf16[736,2152]{1,0:T(8,128)(2,1)} %copy-done.36) | copy-start | bytes 9503236
  484.4 8.1 %copy-start.40 = (bf16[736,2152]{1,0:T(8,128)(2,1)S(1)}, bf16[736,2152]{1,0:T(8,128)(2,1)}, u32[]{:S(2)}) copy-start(bf16[736,2152]{1,0:T(8,128)(2,1)} %copy-done.38) | copy-start | bytes 9503236
  484.4 21.3 %collective-permute-start.7 = (bf16[368,1152]{1,0:T(8,128)(2,1)}, bf16[368,1152]{1,0:T(8,128)(2,1)}, u32[]{:S(2)}, u32[]{:S(2)}) collective-permute-start(bf16[368,1152]{1,0:T(8,128)(2,1)} %convolution_convert_fusion.7), channel_id=1, source_target_pairs={{0,1},{1,0},{2,3},{3,2},{4,5},{5,4},{6,7},{7,6},{8,9},{9,8},{10,11... | collective-permute-start | bytes 2543624 | tf_op jit(solution)/shard_map/ppermute | solution.py:113
  492.0 13.7 %copy-start.71 = (f32[1152]{0:T(1024)S(1)}, f32[1152]{0:T(1024)}, u32[]{:S(2)}) copy-start(f32[1152]{0:T(1024)} %get-tuple-element.57) | copy-start | bytes 13828
  492.0 22.8 %collective-permute-start.3 = (bf16[368,1152]{1,0:T(8,128)(2,1)}, bf16[368,1152]{1,0:T(8,128)(2,1)}, u32[]{:S(2)}, u32[]{:S(2)}) collective-permute-start(bf16[368,1152]{1,0:T(8,128)(2,1)} %convolution_convert_fusion.9), channel_id=1, source_target_pairs={{0,1},{1,0},{2,3},{3,2},{4,5},{5,4},{6,7},{7,6},{8,9},{9,8},{10,11... | collective-permute-start | bytes 2543624 | tf_op jit(solution)/shard_map/ppermute | solution.py:113
  505.6 9.1 %copy-start.82 = (bf16[736,2152]{1,0:T(8,128)(2,1)S(1)}, bf16[736,2152]{1,0:T(8,128)(2,1)}, u32[]{:S(2)}) copy-start(bf16[736,2152]{1,0:T(8,128)(2,1)} %get-tuple-element.103) | copy-start | bytes 9503236
  528.7 28.6 %collective-permute-start.15 = (bf16[368,1152]{1,0:T(8,128)(2,1)S(1)}, bf16[368,1152]{1,0:T(8,128)(2,1)S(1)}, u32[]{:S(2)}, u32[]{:S(2)}) collective-permute-start(bf16[368,1152]{1,0:T(8,128)(2,1)S(1)} %convolution_convert_fusion.3), channel_id=1, source_target_pairs={{0,1},{1,0},{2,3},{3,2},{4,5},{5,4},{6,7},{7,6},{8,9},{9,8},{10,11... | collective-permute-start | bytes 2543624 | tf_op jit(solution)/shard_map/ppermute | solution.py:113
  533.1 26.3 %collective-permute-start.13 = (bf16[368,1152]{1,0:T(8,128)(2,1)S(1)}, bf16[368,1152]{1,0:T(8,128)(2,1)S(1)}, u32[]{:S(2)}, u32[]{:S(2)}) collective-permute-start(bf16[368,1152]{1,0:T(8,128)(2,1)S(1)} %convolution_convert_fusion.4), channel_id=1, source_target_pairs={{0,1},{1,0},{2,3},{3,2},{4,5},{5,4},{6,7},{7,6},{8,9},{9,8},{10,11... | collective-permute-start | bytes 2543624 | tf_op jit(solution)/shard_map/ppermute | solution.py:113
  559.4 46.3 %copy-start.6 = (f32[368,1152]{1,0:T(8,128)S(1)}, f32[368,1152]{1,0:T(8,128)}, u32[]{:S(2)}) copy-start(f32[368,1152]{1,0:T(8,128)} %copy-done.5) | copy-start | bytes 5087236
  (46 other events, 156.5 us)
Sparse Core Ops, SparseCore 0:
  10.9 52.9 all-gather.4
  66.1 37.8 all-gather.6
  106.1 53.7 all-gather.8
  161.8 53.4 all-gather.10
  439.3 57.4 reduce-scatter.12
  500.6 70.9 reduce-scatter.10
  575.6 77.1 reduce-scatter.16
  657.4 76.7 reduce-scatter.14
where the time goes:
time: 747 us; the launch traced here: 743 us
  waiting for transfers between devices  264 us (35%)
  matrix products  253 us (34%)
  other arithmetic  96.3 us (13%)
  local copies, waits for them, and re-layouts  58.3 us (8%)
  blocking collectives  39.7 us (5%)
  starting transfers between devices  16.3 us (2%)
  between operations  15.7 us (2%)
    dot_general x28, matrix products, dot(): lax.dot_general(left, right, (dims, ((), ())), preferred_element_type=jnp...  163 us
    unnamed x11, waiting for transfers between devices  120 us
    ppermute x16, waiting for transfers between devices, swap_halves(): return lax.ppermute(block, 'tp', [(0, 1), (1, 0)])  119 us
    psum x1, blocking collectives, per_device(): total = lax.psum(jnp.concatenate(pieces), ('fsdp', 'tp'))  39.7 us
    convert_element_type x4, local copies, waits for them, and re-layouts, by_shard(): whole.astype(jnp.bfloat16)  26.2 us
    convert_element_type x2, other arithmetic, attend_backward(): d_scores = (probs_full * (d_probs - row_inner)).astype(jnp.bfloat16)  25.8 us
    all_gather x4, waiting for transfers between devices, gather_weight(): return lax.all_gather(shard, 'fsdp', axis=0, tiled=True)  24.9 us
    dot_general x2, matrix products, attend_backward(): jnp.einsum('qhe,khe->hqk', grad_heads, value_heads, preferred_element_typ...  23.6 us
  transfers between devices with their start and end apart: 24, of which 11 were waited for; matrix products, arithmetic and copies ran while one was open for 48% of the time, Pallas kernels for 0%

commit v1 on v0

--- a/solution.py
+++ b/solution.py
@@ -8,6 +8,28 @@
 VALID = 729
 norm_eps = 1e-06
 gelu_coef = math.sqrt(2.0 / math.pi)
+
+
+def joined_along(pieces, dim):
+    pieces = jnp.moveaxis(pieces, 0, dim)
+    dims = pieces.shape
+    return pieces.reshape(*dims[:dim], dims[dim] * dims[dim + 1], *dims[dim + 2 :])
+
+
+def collect(x, axis, dim):
+    size = lax.axis_size(axis)
+    pairs = [(i, (i + 1) % size) for i in range(size)]
+    back = [(b, a) for a, b in pairs]
+    lower, upper = ([], [])
+    for lap in range(size - 1):
+        if lap % 2 == 0:
+            lower.append(lax.ppermute(lower[-1] if lower else x, axis, pairs))
+        else:
+            upper.append(lax.ppermute(upper[-1] if upper else x, axis, back))
+    pieces = jnp.stack([*lower[::-1], x, *upper])
+    shift = lax.axis_index(axis) - len(lower)
+    pieces = pieces[(jnp.arange(size) - shift) % size]
+    return joined_along(pieces, dim)
 
 
 def norm_forward(values, scale_row, shift_row):
@@ -130,7 +152,7 @@
 
 
 def gather_weight(shard):
-    return lax.all_gather(shard, "fsdp", axis=0, tiled=True)
+    return collect(shard, "fsdp", 0)
 
 
 def scatter_weight(whole):

time: 747 us -> 906 us (1.21)
  starting transfers between devices: 16.3 us -> 122 us
  local copies, waits for them, and re-layouts: 58.3 us -> 144 us
  waiting for transfers between devices: 264 us -> 232 us
    ppermute x0 -> x60, starting transfers between devices: none -> 99.6 us  [the longest x28 76.2 us: collect(): upper.append(lax.ppermute(upper[-1] if upper else x, axis, back))]
    unnamed x176 -> x290, local copies, waits for them, and re-layouts: 7.06 us -> 65.2 us
    ppermute x16, waiting for transfers between devices: 119 us -> 63.3 us  [swap_halves(): return lax.ppermute(block, 'tp', [(0, 1), (1, 0)])]
    ppermute x0 -> x60, waiting for transfers between devices: none -> 54.1 us  [the longest x32 47.3 us: collect(): lower.append(lax.ppermute(lower[-1] if lower else x, axis, pairs))]
    all_gather x4 -> x0, waiting for transfers between devices: 24.9 us -> none  [gather_weight(): return lax.all_gather(shard, 'fsdp', axis=0, tiled=True)]
    gather x0 -> x4, local copies, waits for them, and re-layouts: none -> 18.5 us  [collect(): pieces = pieces[(jnp.arange(size) - shift) % size]]
    unnamed x11 -> x7, waiting for transfers between devices: 120 us -> 114 us
  transfers between devices with their start and end apart: 24 -> 80, of which waited for: 11 -> 25; matrix products, arithmetic and copies ran while one was open for 48% -> 49% of each run, Pallas kernels for 0% -> 0%
where the time goes in v1:
time: 906 us; the launch traced here: 896 us
  matrix products  248 us (27%)
  waiting for transfers between devices  232 us (26%)
  local copies, waits for them, and re-layouts  144 us (16%)
  starting transfers between devices  122 us (13%)
  other arithmetic  97.6 us (11%)
  blocking collectives  37.4 us (4%)
  between operations  16 us (2%)
    dot_general x28, matrix products, dot(): lax.dot_general(left, right, (dims, ((), ())), preferred_element_type=jnp...  158 us
    unnamed x7, waiting for transfers between devices  114 us
    ppermute x28, starting transfers between devices, collect(): upper.append(lax.ppermute(upper[-1] if upper else x, axis, back))  76.2 us
    unnamed x290, local copies, waits for them, and re-layouts  65.2 us
    ppermute x16, waiting for transfers between devices, swap_halves(): return lax.ppermute(block, 'tp', [(0, 1), (1, 0)])  63.3 us
    ppermute x32, waiting for transfers between devices, collect(): lower.append(lax.ppermute(lower[-1] if lower else x, axis, pairs))  47.3 us
    psum x1, blocking collectives, per_device(): total = lax.psum(jnp.concatenate(pieces), ('fsdp', 'tp'))  37.4 us
    convert_element_type x4, local copies, waits for them, and re-layouts, by_shard(): whole.astype(jnp.bfloat16)  25.9 us
  transfers between devices with their start and end apart: 80, of which 25 were waited for; matrix products, arithmetic and copies ran while one was open for 49% of the time, Pallas kernels for 0%

profile of v1, /device:TPU:0, one launch (start us, length us, event | category | flops | bytes accessed | tf_op | source)
XLA Modules:
  0.0 896.2 jit_solution(12138512964483418607)
XLA Ops:
  7.3 5.5 collective-permute-start.24
  16.5 4.4 collective-permute-start.9
  21.0 4.4 collective-permute-start.56
  30.1 6.6 collective-permute-done.17
  36.8 6.6 collective-permute-done.18
  45.3 4.9 collective-permute-done.19
  51.6 4.5 collective-permute-start.25
  60.9 4.4 collective-permute-start.26
  67.5 4.6 collective-permute-start.27
  74.2 4.6 collective-permute-start.28
  83.1 5.0 collective-permute-done.3
  90.0 6.6 collective-permute-done.4
  97.6 7.5 collective-permute-done.5
  106.2 4.4 collective-permute-start.41
  116.3 4.6 collective-permute-start.30
  123.4 4.3 collective-permute-start.13
  129.7 4.5 collective-permute-start.42
  171.6 4.4 collective-permute-start.15
  184.1 4.8 collective-permute-start.52
  192.3 5.0 gather_fusion
  200.9 5.2 collective-permute-start.38
  206.1 6.0 add_convert_fusion
  224.3 6.3 add_convert_fusion.1
  239.1 9.4 %fusion.187 = (f32[8,736]{1,0:T(8,128)S(1)}, f32[8,736,736]{1,2,0:T(8,128)}) fusion(bf16[736,8,72]{0,2,1:T(8,128)(2,1)} %bitcast.351, bf16[736,8,72]{0,2,1:T(8,128)(2,1)S(1)} %bitcast.341, pred[736]{0:T(1024)(128)(4,1)S(1)} %copy-done.107), kind=kOutput, calls=%fused_computation.364 | convolution fusion | flops 637028608 | bytes 19054304 | tf_op jit(solution)/shard_map/qhe,khe->hqk/dot_general | solution.py:72
  248.4 8.8 fusion
  257.2 9.1 %fusion.147 = bf16[8,72,736]{2,1,0:T(8,128)(2,1)} fusion(bf16[736,8,72]{0,2,1:T(8,128)(2,1)S(1)} %bitcast.382, f32[8,736,736]{1,2,0:T(8,128)} %get-tuple-element.106, f32[8,736]{1,0:T(8,128)S(1)} %fusion, f32[8,736]{1,0:T(8,128)S(1)} %get-tuple-element.105), kind=kOutput, calls=%fused_computation.219 | convolution fusion | flops 637458432 | bytes 19077120 | tf_op jit(solution)/shard_map/hqk,khe->qhe/dot_general | solution.py:86
  266.3 8.3 fusion.186
  274.6 8.8 fusion.1
  283.4 8.7 fusion.146
  315.6 4.7 collective-permute-start.31
  342.2 17.7 %collective-permute-done.65 = bf16[368,1152]{1,0:T(8,128)(2,1)S(1)} collective-permute-done((bf16[368,1152]{1,0:T(8,128)(2,1)S(1)}, bf16[368,1152]{1,0:T(8,128)(2,1)S(1)}, u32[]{:S(2)}, u32[]{:S(2)}) %collective-permute-start.65) | collective-permute-done | bytes 847904 | tf_op jit(solution)/shard_map/ppermute | solution.py:135
  365.9 5.9 gather_fusion.2
  373.6 5.8 gather_fusion.3
  379.4 5.6 collective-permute-done.66
  384.9 10.0 %fusion.120 = f32[736,2152]{1,0:T(8,128)} fusion(bf16[1152,2152]{1,0:T(8,128)(2,1)} %bitcast.366, bf16[368,1152]{1,0:T(8,128)(2,1)} %collective-permute-done.66, bf16[368,1152]{1,0:T(8,128)(2,1)S(1)} %get-tuple-element.96), kind=kOutput, calls=%fused_computation.175 | convolution fusion | flops 3652632576 | bytes 12989440 | tf_op jit(solution)/shard_map/dot_general | solution.py:126
  395.0 9.7 %fusion.27 = bf16[736,2152]{1,0:T(8,128)(2,1)S(1)} fusion(bf16[1152,2152]{1,0:T(8,128)(2,1)S(1)} %bitcast.364, f32[736,2152]{1,0:T(8,128)} %fusion.120, f32[2152]{0:T(1024)S(1)} %dynamic_slice.17, bf16[368,1152]{1,0:T(8,128)(2,1)} %collective-permute-done.69, bf16[368,1152]{1,0:T(8,128)(2,1)} %get-tuple-element.80), kind=kOutput, calls=%fused_computation.50 | convolution fusion | flops 3684310016 | bytes 16165792 | tf_op jit(solution)/shard_map/dot_general | solution.py:126
  410.1 11.3 %multiply_convert_fusion.3 = (bf16[736,2152]{1,0:T(8,128)(2,1)S(1)}, bf16[736,2152]{1,0:T(8,128)(2,1)}, f32[736,2152]{1,0:T(8,128)}) fusion(f32[2152]{0:T(1024)S(1)} %dynamic_slice.17, f32[736,2152]{1,0:T(8,128)} %fusion.120, bf16[1152,2152]{1,0:T(8,128)(2,1)S(1)} %bitcast.372, bf16[368,1152]{1,0:T(8,128)(2,1)S(1)} %collective-permute-done.32, ...), kind=kOutput, calls=%fused_computation.56 | convolution fusion | flops 3684310016 | bytes 25669024 | tf_op jit(solution)/shard_map/dot_general | solution.py:126
  421.4 10.6 %fusion.21 = bf16[736,2152]{1,0:T(8,128)(2,1)S(1)} fusion(bf16[1152,2152]{1,0:T(8,128)(2,1)S(1)} %bitcast.365, f32[736,2152]{1,0:T(8,128)} %get-tuple-element.111, f32[2152]{0:T(1024)S(1)} %dynamic_slice.17, bf16[368,1152]{1,0:T(8,128)(2,1)} %collective-permute-done.68, bf16[368,1152]{1,0:T(8,128)(2,1)S(1)} %copy-done.49), kind=kOutput, calls=%fused_computation.44 | convolution fusion | flops 3684310016 | bytes 16165792 | tf_op jit(solution)/shard_map/dot_general | solution.py:126
  435.4 13.5 %convolution_convert_fusion = bf16[1152,2152]{0,1:T(8,128)(2,1)} fusion(bf16[736,2152]{1,0:T(8,128)(2,1)S(1)} %fusion.27, bf16[736,2152]{1,0:T(8,128)(2,1)S(1)} %fusion.21, bf16[368,1152]{1,0:T(8,128)(2,1)} %collective-permute-done.66, bf16[368,1152]{1,0:T(8,128)(2,1)S(1)} %get-tuple-element.96, bf16[368,1152]{1,0:T(8,128)(2,1)S(1)} %collective-permute-done.32, ...), kind=kOutput, calls=%fused_computation.21 | convolution fusion | flops 7327198208 | bytes 14685184 | tf_op jit(solution)/shard_map/dot_general | solution.py:126
  448.9 14.1 %convolution_convert_fusion.1 = bf16[1152,2152]{0,1:T(8,128)(2,1)} fusion(bf16[736,2152]{1,0:T(8,128)(2,1)} %get-tuple-element.98, bf16[736,2152]{1,0:T(8,128)(2,1)S(1)} %get-tuple-element.97, bf16[368,1152]{1,0:T(8,128)(2,1)} %collective-permute-done.69, bf16[368,1152]{1,0:T(8,128)(2,1)} %get-tuple-element.80, ...), kind=kOutput, calls=%fused_computation.22 | convolution fusion | flops 7327198208 | bytes 14685184 | tf_op jit(solution)/shard_map/dot_general | solution.py:126
  463.0 8.4 copy.73
  471.4 8.4 copy.72
  479.9 6.8 convolution_add_fusion.4
  486.7 6.4 convolution_add_fusion.5
  501.9 19.6 %collective-permute-done.74 = bf16[368,1152]{1,0:T(8,128)(2,1)S(1)} collective-permute-done((bf16[368,1152]{1,0:T(8,128)(2,1)S(1)}, bf16[368,1152]{1,0:T(8,128)(2,1)S(1)}, u32[]{:S(2)}, u32[]{:S(2)}) %collective-permute-start.74) | collective-permute-done | bytes 847904 | tf_op jit(solution)/shard_map/ppermute | solution.py:135
  522.9 11.6 %multiply_reduce_fusion = (f32[8,736]{1,0:T(8,128)S(1)}, f32[8,736,736]{1,2,0:T(8,128)}) fusion(f32[8,736,736]{1,2,0:T(8,128)} %get-tuple-element.104, f32[8,736]{1,0:T(8,128)S(1)} %log_add_fusion, bf16[736,8,72]{0,2,1:T(8,128)(2,1)S(1)} %bitcast.384, bf16[736,8,72]{0,2,1:T(8,128)(2,1)S(1)} %bitcast.381), kind=kOutput, calls=%fused_computation.5 | convolution fusion | flops 637028608 | bytes 36411392 | tf_op jit(solution)/shard_map/qhe,khe->hqk/dot_general | solution.py:99
  534.5 12.6 %multiply_convert_fusion = bf16[8,736,736]{1,2,0:T(8,128)(2,1)S(1)} fusion(f32[8,736,736]{1,2,0:T(8,128)} %get-tuple-element.115, f32[8,736,736]{1,2,0:T(8,128)} %get-tuple-element.104, f32[8,736]{1,0:T(8,128)S(1)} %get-tuple-element.114, f32[8,736]{1,0:T(8,128)S(1)} %log_add_fusion), kind=kLoop, calls=%fused_computation.4 | loop fusion | flops 17334272 | bytes 43382784 | tf_op jit(solution)/shard_map/convert_element_type | solution.py:103
  553.4 9.9 %fusion.151 = bf16[8,72,736]{2,1,0:T(8,128)(2,1)} fusion(bf16[736,8,72]{0,2,1:T(8,128)(2,1)S(1)} %bitcast.385, f32[8,736,736]{1,2,0:T(8,128)} %get-tuple-element.104, f32[8,736]{1,0:T(8,128)S(1)} %log_add_fusion), kind=kOutput, calls=%fused_computation.221 | convolution fusion | flops 633124864 | bytes 19053568 | tf_op jit(solution)/shard_map/hqk,qhe->khe/dot_general | solution.py:104
  564.8 9.9 %fusion.148 = bf16[8,72,736]{2,1,0:T(8,128)(2,1)} fusion(bf16[736,8,72]{0,2,1:T(8,128)(2,1)S(1)} %bitcast.386, f32[8,736,736]{1,2,0:T(8,128)} %get-tuple-element.106, f32[8,736]{1,0:T(8,128)S(1)} %log_add_fusion.1), kind=kOutput, calls=%fused_computation.220 | convolution fusion | flops 633124864 | bytes 19053568 | tf_op jit(solution)/shard_map/hqk,qhe->khe/dot_general | solution.py:104
  574.7 12.0 %multiply_reduce_fusion.1 = (f32[8,736]{1,0:T(8,128)S(1)}, f32[8,736,736]{1,2,0:T(8,128)}) fusion(f32[8,736,736]{1,2,0:T(8,128)} %get-tuple-element.106, f32[8,736]{1,0:T(8,128)S(1)} %log_add_fusion.1, bf16[736,8,72]{0,2,1:T(8,128)(2,1)S(1)} %bitcast.387, bf16[736,8,72]{0,2,1:T(8,128)(2,1)S(1)} %bitcast.383), kind=kOutput, calls=%fused_computation.8 | convolution fusion | flops 637028608 | bytes 36411392 | tf_op jit(solution)/shard_map/qhe,khe->hqk/dot_general | solution.py:99
  593.0 13.2 %multiply_convert_fusion.1 = bf16[8,736,736]{1,2,0:T(8,128)(2,1)S(1)} fusion(f32[8,736,736]{1,2,0:T(8,128)} %get-tuple-element.113, f32[8,736,736]{1,2,0:T(8,128)} %get-tuple-element.106, f32[8,736]{1,0:T(8,128)S(1)} %get-tuple-element.112, f32[8,736]{1,0:T(8,128)S(1)} %log_add_fusion.1), kind=kLoop, calls=%fused_computation.7 | loop fusion | flops 17334272 | bytes 43382784 | tf_op jit(solution)/shard_map/convert_element_type | solution.py:103
  611.7 10.9 %convolution_convert_fusion.2 = bf16[1152,1728]{0,1:T(8,128)(2,1)} fusion(bf16[368,1152]{1,0:T(8,128)(2,1)} %collective-permute-done.64, bf16[368,1152]{1,0:T(8,128)(2,1)S(1)} %copy-done.51, bf16[368,1152]{1,0:T(8,128)(2,1)} %collective-permute-done, bf16[368,1152]{1,0:T(8,128)(2,1)} %get-tuple-element.73, bf16[736,576]{0,1:T(8,128)(2,1)S(1)} %bitcast.354, ...), kind=kOutput, calls=%fused_computation.34 | convolution fusion | flops 5906571264 | bytes 12460032 | tf_op jit(solution)/shard_map/dot_general | solution.py:126
  622.6 6.4 copy.80
  631.8 6.3 convolution_convert_fusion.7
  640.0 5.7 convolution_convert_fusion.9
  647.4 12.8 %collective-permute-done.67 = bf16[368,1152]{1,0:T(8,128)(2,1)} collective-permute-done((bf16[368,1152]{1,0:T(8,128)(2,1)}, bf16[368,1152]{1,0:T(8,128)(2,1)}, u32[]{:S(2)}, u32[]{:S(2)}) %collective-permute-start.67) | collective-permute-done | bytes 847904 | tf_op jit(solution)/shard_map/ppermute | solution.py:135
  660.2 6.1 fusion.73
  666.3 5.6 collective-permute-done.63
  672.0 5.1 fusion.74
  689.7 23.3 %convert_reduce_fusion.1 = f32[1728]{0:T(1024)S(1)} fusion(bf16[736,576]{0,1:T(8,128)(2,1)S(1)} %bitcast.355, bf16[736,576]{0,1:T(8,128)(2,1)S(1)} %bitcast.345, bf16[736,576]{0,1:T(8,128)(2,1)S(1)} %bitcast.335, bf16[736,576]{0,1:T(8,128)(2,1)S(1)} %bitcast.358, bf16[736,576]{0,1:T(8,128)(2,1)S(1)} %bitcast.348, bf16[736,576]{0,1:T(8,128)(2,1)S(1)} %bitcast.338), kind=kLoop, calls=%fused_computation.23 | loop fusion | flops 33065280 | bytes 5094144 | tf_op jit(solution)/shard_map/reduce_sum | solution.py:246
  717.5 4.9 fusion.108
  722.7 37.4 %psum.7 = f32[13520]{0:T(1024)S(1)} all-reduce(f32[13520]{0:T(1024)S(1)} %constant_dynamic-update-slice_fusion.18), channel_id=1, replica_groups=mesh['fsdp'=16,'tp'=2] {'fsdp','tp'}, use_global_device_ids=true, to_apply=%region_39.40 | all-reduce | flops 13520 | bytes 108160 | tf_op jit(solution)/shard_map/psum | solution.py:274
  772.2 33.8 %reduce-scatter.17.cloned.1.call-done = bf16[1,72,2152]{2,1,0:T(8,128)(2,1)} async-done(((bf16[16,72,2152]{2,1,0:T(8,128)(2,1)}), bf16[1,72,2152]{2,1,0:T(8,128)(2,1)}) %reduce-scatter.17.cloned.1.call-update) | async-done | bytes 309904
  807.9 79.5 %reduce-scatter.15.cloned.1.call-done = bf16[1,72,2152]{2,1,0:T(8,128)(2,1)} async-done(((bf16[16,72,2152]{2,1,0:T(8,128)(2,1)}), bf16[1,72,2152]{2,1,0:T(8,128)(2,1)}) %reduce-scatter.15.cloned.1.call-update) | async-done | bytes 309904
  (535 shorter events, 242.2 us)
Async XLA Ops:
  7.2 761.3 %reduce-scatter.13.cloned.1.call-start = ((), (), s32[]{:S(2)}) async-start(), calls=%async_computation.5 | async-start | bytes 1566720
  7.3 44.3 %collective-permute-start.24 = (bf16[72,576]{1,0:T(8,128)(2,1)}, bf16[72,576]{1,0:T(8,128)(2,1)}, u32[]{:S(2)}, u32[]{:S(2)}) collective-permute-start(bf16[72,576]{1,0:T(8,128)(2,1)} %bitcast.406), channel_id=1, source_target_pairs={{2,0},{4,2},{6,4},{8,6},{10,8},{12,10},{14,12},{16,14},{18,16},{20... | collective-permute-start | bytes 248840 | tf_op jit(solution)/shard_map/ppermute | solution.py:28
  12.7 17.2 %collective-permute-start.16 = (bf16[72,576]{1,0:T(8,128)(2,1)}, bf16[72,576]{1,0:T(8,128)(2,1)S(1)}, u32[]{:S(2)}, u32[]{:S(2)}) collective-permute-start(bf16[72,576]{1,0:T(8,128)(2,1)} %bitcast.407), channel_id=1, source_target_pairs={{0,2},{2,4},{4,6},{6,8},{8,10},{10,12},{12,14},{14,16},{16,18},{18... | collective-permute-start | bytes 248840 | tf_op jit(solution)/shard_map/ppermute | solution.py:26
  16.5 39.6 %collective-permute-start.9 = (bf16[72,1728]{1,0:T(8,128)(2,1)}, bf16[72,1728]{1,0:T(8,128)(2,1)}, u32[]{:S(2)}, u32[]{:S(2)}) collective-permute-start(bf16[72,1728]{1,0:T(8,128)(2,1)} %reshape.279), channel_id=1, source_target_pairs={{2,0},{4,2},{6,4},{8,6},{10,8},{12,10},{14,12},{16,14},{18,16},{20... | collective-permute-start | bytes 746504 | tf_op jit(solution)/shard_map/ppermute | solution.py:28
  21.0 35.2 %collective-permute-start.1 = (bf16[72,1728]{1,0:T(8,128)(2,1)}, bf16[72,1728]{1,0:T(8,128)(2,1)}, u32[]{:S(2)}, u32[]{:S(2)}) collective-permute-start(bf16[72,1728]{1,0:T(8,128)(2,1)} %reshape.279), channel_id=1, source_target_pairs={{0,2},{2,4},{4,6},{6,8},{8,10},{10,12},{12,14},{14,16},{16,18},{18... | collective-permute-start | bytes 746504 | tf_op jit(solution)/shard_map/ppermute | solution.py:26
  21.0 85.2 %collective-permute-start.56 = (bf16[72,2152]{1,0:T(8,128)(2,1)}, bf16[72,2152]{1,0:T(8,128)(2,1)}, u32[]{:S(2)}, u32[]{:S(2)}) collective-permute-start(bf16[72,2152]{1,0:T(8,128)(2,1)} %bitcast.403), channel_id=1, source_target_pairs={{2,0},{4,2},{6,4},{8,6},{10,8},{12,10},{14,12},{16,14},{18,16},{20... | collective-permute-start | bytes 929672 | tf_op jit(solution)/shard_map/ppermute | solution.py:28
  51.6 9.3 %collective-permute-start.25 = (bf16[72,576]{1,0:T(8,128)(2,1)}, bf16[72,576]{1,0:T(8,128)(2,1)S(1)}, u32[]{:S(2)}, u32[]{:S(2)}) collective-permute-start(bf16[72,576]{1,0:T(8,128)(2,1)} %collective-permute-done.24), channel_id=1, source_target_pairs={{2,0},{4,2},{6,4},{8,6},{10,8},{12,10},{14,12},{16,14},{18,16},{20... | collective-permute-start | bytes 248840 | tf_op jit(solution)/shard_map/ppermute | solution.py:28
  56.1 18.2 %collective-permute-start.10 = (bf16[72,1728]{1,0:T(8,128)(2,1)}, bf16[72,1728]{1,0:T(8,128)(2,1)}, u32[]{:S(2)}, u32[]{:S(2)}) collective-permute-start(bf16[72,1728]{1,0:T(8,128)(2,1)} %collective-permute-done.9), channel_id=1, source_target_pairs={{2,0},{4,2},{6,4},{8,6},{10,8},{12,10},{14,12},{16,14},{18,16},{20... | collective-permute-start | bytes 746504 | tf_op jit(solution)/shard_map/ppermute | solution.py:28
  56.2 22.7 %collective-permute-start.2 = (bf16[72,1728]{1,0:T(8,128)(2,1)}, bf16[72,1728]{1,0:T(8,128)(2,1)}, u32[]{:S(2)}, u32[]{:S(2)}) collective-permute-start(bf16[72,1728]{1,0:T(8,128)(2,1)} %collective-permute-done.1), channel_id=1, source_target_pairs={{0,2},{2,4},{4,6},{6,8},{8,10},{10,12},{12,14},{14,16},{16,18},{18... | collective-permute-start | bytes 746504 | tf_op jit(solution)/shard_map/ppermute | solution.py:26
  74.2 32.0 %collective-permute-start.48 = (bf16[72,2152]{1,0:T(8,128)(2,1)}, bf16[72,2152]{1,0:T(8,128)(2,1)}, u32[]{:S(2)}, u32[]{:S(2)}) collective-permute-start(bf16[72,2152]{1,0:T(8,128)(2,1)} %bitcast.404), channel_id=1, source_target_pairs={{0,2},{2,4},{4,6},{6,8},{8,10},{10,12},{12,14},{14,16},{16,18},{18... | collective-permute-start | bytes 929672 | tf_op jit(solution)/shard_map/ppermute | solution.py:26
  74.2 36.4 %collective-permute-start.28 = (bf16[72,576]{1,0:T(8,128)(2,1)S(1)}, bf16[72,576]{1,0:T(8,128)(2,1)S(1)}, u32[]{:S(2)}, u32[]{:S(2)}) collective-permute-start(bf16[72,576]{1,0:T(8,128)(2,1)S(1)} %collective-permute-done.27), channel_id=1, source_target_pairs={{2,0},{4,2},{6,4},{8,6},{10,8},{12,10},{14,12},{16,14},{18,16},{20... | collective-permute-start | bytes 248840 | tf_op jit(solution)/shard_map/ppermute | solution.py:28
  78.9 32.2 %collective-permute-start.11 = (bf16[72,1728]{1,0:T(8,128)(2,1)}, bf16[72,1728]{1,0:T(8,128)(2,1)S(1)}, u32[]{:S(2)}, u32[]{:S(2)}) collective-permute-start(bf16[72,1728]{1,0:T(8,128)(2,1)} %collective-permute-done.10), channel_id=1, source_target_pairs={{2,0},{4,2},{6,4},{8,6},{10,8},{12,10},{14,12},{16,14},{18,16},{20... | collective-permute-start | bytes 746504 | tf_op jit(solution)/shard_map/ppermute | solution.py:28
  106.1 14.8 %collective-permute-start.33 = (bf16[72,2152]{1,0:T(8,128)(2,1)}, bf16[72,2152]{1,0:T(8,128)(2,1)}, u32[]{:S(2)}, u32[]{:S(2)}) collective-permute-start(bf16[72,2152]{1,0:T(8,128)(2,1)} %param.12), channel_id=1, source_target_pairs={{0,2},{2,4},{4,6},{6,8},{8,10},{10,12},{12,14},{14,16},{16,18},{18... | collective-permute-start | bytes 929672 | tf_op jit(solution)/shard_map/ppermute | solution.py:26
  106.2 14.8 %collective-permute-start.41 = (bf16[72,2152]{1,0:T(8,128)(2,1)}, bf16[72,2152]{1,0:T(8,128)(2,1)S(1)}, u32[]{:S(2)}, u32[]{:S(2)}) collective-permute-start(bf16[72,2152]{1,0:T(8,128)(2,1)} %param.12), channel_id=1, source_target_pairs={{2,0},{4,2},{6,4},{8,6},{10,8},{12,10},{14,12},{16,14},{18,16},{20... | collective-permute-start | bytes 929672 | tf_op jit(solution)/shard_map/ppermute | solution.py:28
  111.1 12.3 %collective-permute-start.12 = (bf16[72,1728]{1,0:T(8,128)(2,1)S(1)}, bf16[72,1728]{1,0:T(8,128)(2,1)}, u32[]{:S(2)}, u32[]{:S(2)}) collective-permute-start(bf16[72,1728]{1,0:T(8,128)(2,1)S(1)} %collective-permute-done.11), channel_id=1, source_target_pairs={{2,0},{4,2},{6,4},{8,6},{10,8},{12,10},{14,12},{16,14},{18,16},{20... | collective-permute-start | bytes 746504 | tf_op jit(solution)/shard_map/ppermute | solution.py:28
  113.7 14.0 %collective-permute-start.7 = (bf16[72,1728]{1,0:T(8,128)(2,1)S(1)}, bf16[72,1728]{1,0:T(8,128)(2,1)}, u32[]{:S(2)}, u32[]{:S(2)}) collective-permute-start(bf16[72,1728]{1,0:T(8,128)(2,1)S(1)} %collective-permute-done.6), channel_id=1, source_target_pairs={{0,2},{2,4},{4,6},{6,8},{8,10},{10,12},{12,14},{14,16},{16,18},{18... | collective-permute-start | bytes 746504 | tf_op jit(solution)/shard_map/ppermute | solution.py:26
  121.0 13.2 %collective-permute-start.49 = (bf16[72,2152]{1,0:T(8,128)(2,1)}, bf16[72,2152]{1,0:T(8,128)(2,1)}, u32[]{:S(2)}, u32[]{:S(2)}) collective-permute-start(bf16[72,2152]{1,0:T(8,128)(2,1)} %collective-permute-done.48), channel_id=1, source_target_pairs={{0,2},{2,4},{4,6},{6,8},{8,10},{10,12},{12,14},{14,16},{16,18},{18... | collective-permute-start | bytes 929672 | tf_op jit(solution)/shard_map/ppermute | solution.py:26
  123.0 14.0 %collective-permute-start.34 = (bf16[72,2152]{1,0:T(8,128)(2,1)}, bf16[72,2152]{1,0:T(8,128)(2,1)}, u32[]{:S(2)}, u32[]{:S(2)}) collective-permute-start(bf16[72,2152]{1,0:T(8,128)(2,1)} %collective-permute-done.33), channel_id=1, source_target_pairs={{0,2},{2,4},{4,6},{6,8},{8,10},{10,12},{12,14},{14,16},{16,18},{18... | collective-permute-start | bytes 929672 | tf_op jit(solution)/shard_map/ppermute | solution.py:26
  123.4 17.1 %collective-permute-start.13 = (bf16[72,1728]{1,0:T(8,128)(2,1)}, bf16[72,1728]{1,0:T(8,128)(2,1)}, u32[]{:S(2)}, u32[]{:S(2)}) collective-permute-start(bf16[72,1728]{1,0:T(8,128)(2,1)} %collective-permute-done.12), channel_id=1, source_target_pairs={{2,0},{4,2},{6,4},{8,6},{10,8},{12,10},{14,12},{16,14},{18,16},{20... | collective-permute-start | bytes 746504 | tf_op jit(solution)/shard_map/ppermute | solution.py:28
  127.7 15.3 %collective-permute-start.8 = (bf16[72,1728]{1,0:T(8,128)(2,1)}, bf16[72,1728]{1,0:T(8,128)(2,1)}, u32[]{:S(2)}, u32[]{:S(2)}) collective-permute-start(bf16[72,1728]{1,0:T(8,128)(2,1)} %collective-permute-done.7), channel_id=1, source_target_pairs={{0,2},{2,4},{4,6},{6,8},{8,10},{10,12},{12,14},{14,16},{16,18},{18... | collective-permute-start | bytes 746504 | tf_op jit(solution)/shard_map/ppermute | solution.py:26
  129.7 36.8 %collective-permute-start.42 = (bf16[72,2152]{1,0:T(8,128)(2,1)}, bf16[72,2152]{1,0:T(8,128)(2,1)S(1)}, u32[]{:S(2)}, u32[]{:S(2)}) collective-permute-start(bf16[72,2152]{1,0:T(8,128)(2,1)} %copy-done.54), channel_id=1, source_target_pairs={{2,0},{4,2},{6,4},{8,6},{10,8},{12,10},{14,12},{16,14},{18,16},{20... | collective-permute-start | bytes 929672 | tf_op jit(solution)/shard_map/ppermute | solution.py:28
  134.2 33.8 %collective-permute-start.58 = (bf16[72,2152]{1,0:T(8,128)(2,1)}, bf16[72,2152]{1,0:T(8,128)(2,1)S(1)}, u32[]{:S(2)}, u32[]{:S(2)}) collective-permute-start(bf16[72,2152]{1,0:T(8,128)(2,1)} %collective-permute-done.57), channel_id=1, source_target_pairs={{2,0},{4,2},{6,4},{8,6},{10,8},{12,10},{14,12},{16,14},{18,16},{20... | collective-permute-start | bytes 929672 | tf_op jit(solution)/shard_map/ppermute | solution.py:28
  137.0 34.5 %collective-permute-start.50 = (bf16[72,2152]{1,0:T(8,128)(2,1)}, bf16[72,2152]{1,0:T(8,128)(2,1)S(1)}, u32[]{:S(2)}, u32[]{:S(2)}) collective-permute-start(bf16[72,2152]{1,0:T(8,128)(2,1)} %collective-permute-done.49), channel_id=1, source_target_pairs={{0,2},{2,4},{4,6},{6,8},{8,10},{10,12},{12,14},{14,16},{16,18},{18... | collective-permute-start | bytes 929672 | tf_op jit(solution)/shard_map/ppermute | solution.py:26
  140.5 31.0 %collective-permute-start.35 = (bf16[72,2152]{1,0:T(8,128)(2,1)}, bf16[72,2152]{1,0:T(8,128)(2,1)S(1)}, u32[]{:S(2)}, u32[]{:S(2)}) collective-permute-start(bf16[72,2152]{1,0:T(8,128)(2,1)} %collective-permute-done.34), channel_id=1, source_target_pairs={{0,2},{2,4},{4,6},{6,8},{8,10},{10,12},{12,14},{14,16},{16,18},{18... | collective-permute-start | bytes 929672 | tf_op jit(solution)/shard_map/ppermute | solution.py:26
  143.0 28.6 %collective-permute-start.14 = (bf16[72,1728]{1,0:T(8,128)(2,1)}, bf16[72,1728]{1,0:T(8,128)(2,1)S(1)}, u32[]{:S(2)}, u32[]{:S(2)}) collective-permute-start(bf16[72,1728]{1,0:T(8,128)(2,1)} %collective-permute-done.13), channel_id=1, source_target_pairs={{2,0},{4,2},{6,4},{8,6},{10,8},{12,10},{14,12},{16,14},{18,16},{20... | collective-permute-start | bytes 746504 | tf_op jit(solution)/shard_map/ppermute | solution.py:28
  166.4 30.8 %collective-permute-start.64 = (bf16[368,1152]{1,0:T(8,128)(2,1)S(1)}, bf16[368,1152]{1,0:T(8,128)(2,1)}, u32[]{:S(2)}, u32[]{:S(2)}) collective-permute-start(bf16[368,1152]{1,0:T(8,128)(2,1)S(1)} %copy-done.50), channel_id=1, source_target_pairs={{0,1},{1,0},{2,3},{3,2},{4,5},{5,4},{6,7},{7,6},{8,9},{9,8},{10,11... | collective-permute-start | bytes 2543624 | tf_op jit(solution)/shard_map/ppermute | solution.py:135
  168.0 8.8 collective-permute-start.43
  171.5 9.2 %collective-permute-start.51 = (bf16[72,2152]{1,0:T(8,128)(2,1)S(1)}, bf16[72,2152]{1,0:T(8,128)(2,1)S(1)}, u32[]{:S(2)}, u32[]{:S(2)}) collective-permute-start(bf16[72,2152]{1,0:T(8,128)(2,1)S(1)} %collective-permute-done.50), channel_id=1, source_target_pairs={{0,2},{2,4},{4,6},{6,8},{8,10},{10,12},{12,14},{14,16},{16,18},{18... | collective-permute-start | bytes 929672 | tf_op jit(solution)/shard_map/ppermute | solution.py:26
  171.6 12.6 %collective-permute-start.36 = (bf16[72,2152]{1,0:T(8,128)(2,1)S(1)}, bf16[72,2152]{1,0:T(8,128)(2,1)}, u32[]{:S(2)}, u32[]{:S(2)}) collective-permute-start(bf16[72,2152]{1,0:T(8,128)(2,1)S(1)} %collective-permute-done.35), channel_id=1, source_target_pairs={{0,2},{2,4},{4,6},{6,8},{8,10},{10,12},{12,14},{14,16},{16,18},{18... | collective-permute-start | bytes 929672 | tf_op jit(solution)/shard_map/ppermute | solution.py:26
  171.6 17.3 %collective-permute-start.15 = (bf16[72,1728]{1,0:T(8,128)(2,1)S(1)}, bf16[72,1728]{1,0:T(8,128)(2,1)S(1)}, u32[]{:S(2)}, u32[]{:S(2)}) collective-permute-start(bf16[72,1728]{1,0:T(8,128)(2,1)S(1)} %collective-permute-done.14), channel_id=1, source_target_pairs={{2,0},{4,2},{6,4},{8,6},{10,8},{12,10},{14,12},{16,14},{18,16},{20... | collective-permute-start | bytes 746504 | tf_op jit(solution)/shard_map/ppermute | solution.py:28
  176.8 21.0 %collective-permute-start.59 = (bf16[72,2152]{1,0:T(8,128)(2,1)S(1)}, bf16[72,2152]{1,0:T(8,128)(2,1)}, u32[]{:S(2)}, u32[]{:S(2)}) collective-permute-start(bf16[72,2152]{1,0:T(8,128)(2,1)S(1)} %collective-permute-done.58), channel_id=1, source_target_pairs={{2,0},{4,2},{6,4},{8,6},{10,8},{12,10},{14,12},{16,14},{18,16},{20... | collective-permute-start | bytes 929672 | tf_op jit(solution)/shard_map/ppermute | solution.py:28
  180.7 18.7 %collective-permute-start.44 = (bf16[72,2152]{1,0:T(8,128)(2,1)S(1)}, bf16[72,2152]{1,0:T(8,128)(2,1)}, u32[]{:S(2)}, u32[]{:S(2)}) collective-permute-start(bf16[72,2152]{1,0:T(8,128)(2,1)S(1)} %collective-permute-done.43), channel_id=1, source_target_pairs={{2,0},{4,2},{6,4},{8,6},{10,8},{12,10},{14,12},{16,14},{18,16},{20... | collective-permute-start | bytes 929672 | tf_op jit(solution)/shard_map/ppermute | solution.py:28
  184.1 16.7 %collective-permute-start.52 = (bf16[72,2152]{1,0:T(8,128)(2,1)S(1)}, bf16[72,2152]{1,0:T(8,128)(2,1)}, u32[]{:S(2)}, u32[]{:S(2)}) collective-permute-start(bf16[72,2152]{1,0:T(8,128)(2,1)S(1)} %collective-permute-done.51), channel_id=1, source_target_pairs={{0,2},{2,4},{4,6},{6,8},{8,10},{10,12},{12,14},{14,16},{16,18},{18... | collective-permute-start | bytes 929672 | tf_op jit(solution)/shard_map/ppermute | solution.py:26
  188.9 11.9 %collective-permute-start.37 = (bf16[72,2152]{1,0:T(8,128)(2,1)}, bf16[72,2152]{1,0:T(8,128)(2,1)}, u32[]{:S(2)}, u32[]{:S(2)}) collective-permute-start(bf16[72,2152]{1,0:T(8,128)(2,1)} %collective-permute-done.36), channel_id=1, source_target_pairs={{0,2},{2,4},{4,6},{6,8},{8,10},{10,12},{12,14},{14,16},{16,18},{18... | collective-permute-start | bytes 929672 | tf_op jit(solution)/shard_map/ppermute | solution.py:26
  197.2 22.5 %collective-permute-start = (bf16[368,1152]{1,0:T(8,128)(2,1)}, bf16[368,1152]{1,0:T(8,128)(2,1)}, u32[]{:S(2)}, u32[]{:S(2)}) collective-permute-start(bf16[368,1152]{1,0:T(8,128)(2,1)} %get-tuple-element.73), channel_id=1, source_target_pairs={{0,1},{1,0},{2,3},{3,2},{4,5},{5,4},{6,7},{7,6},{8,9},{9,8},{10,11... | collective-permute-start | bytes 2543624 | tf_op jit(solution)/shard_map/ppermute | solution.py:135
  197.8 22.5 %collective-permute-start.60 = (bf16[72,2152]{1,0:T(8,128)(2,1)}, bf16[72,2152]{1,0:T(8,128)(2,1)}, u32[]{:S(2)}, u32[]{:S(2)}) collective-permute-start(bf16[72,2152]{1,0:T(8,128)(2,1)} %collective-permute-done.59), channel_id=1, source_target_pairs={{2,0},{4,2},{6,4},{8,6},{10,8},{12,10},{14,12},{16,14},{18,16},{20... | collective-permute-start | bytes 929672 | tf_op jit(solution)/shard_map/ppermute | solution.py:28
  199.4 21.4 %collective-permute-start.45 = (bf16[72,2152]{1,0:T(8,128)(2,1)}, bf16[72,2152]{1,0:T(8,128)(2,1)}, u32[]{:S(2)}, u32[]{:S(2)}) collective-permute-start(bf16[72,2152]{1,0:T(8,128)(2,1)} %collective-permute-done.44), channel_id=1, source_target_pairs={{2,0},{4,2},{6,4},{8,6},{10,8},{12,10},{14,12},{16,14},{18,16},{20... | collective-permute-start | bytes 929672 | tf_op jit(solution)/shard_map/ppermute | solution.py:28
  200.9 20.7 %collective-permute-start.53 = (bf16[72,2152]{1,0:T(8,128)(2,1)}, bf16[72,2152]{1,0:T(8,128)(2,1)}, u32[]{:S(2)}, u32[]{:S(2)}) collective-permute-start(bf16[72,2152]{1,0:T(8,128)(2,1)} %collective-permute-done.52), channel_id=1, source_target_pairs={{0,2},{2,4},{4,6},{6,8},{8,10},{10,12},{12,14},{14,16},{16,18},{18... | collective-permute-start | bytes 929672 | tf_op jit(solution)/shard_map/ppermute | solution.py:26
  200.9 21.8 %collective-permute-start.38 = (bf16[72,2152]{1,0:T(8,128)(2,1)}, bf16[72,2152]{1,0:T(8,128)(2,1)}, u32[]{:S(2)}, u32[]{:S(2)}) collective-permute-start(bf16[72,2152]{1,0:T(8,128)(2,1)} %collective-permute-done.37), channel_id=1, source_target_pairs={{0,2},{2,4},{4,6},{6,8},{8,10},{10,12},{12,14},{14,16},{16,18},{18... | collective-permute-start | bytes 929672 | tf_op jit(solution)/shard_map/ppermute | solution.py:26
  219.8 201.6 %collective-permute-start.68 = (bf16[368,1152]{1,0:T(8,128)(2,1)}, bf16[368,1152]{1,0:T(8,128)(2,1)}, u32[]{:S(2)}, u32[]{:S(2)}) collective-permute-start(bf16[368,1152]{1,0:T(8,128)(2,1)} %get-tuple-element.79), channel_id=1, source_target_pairs={{0,1},{1,0},{2,3},{3,2},{4,5},{5,4},{6,7},{7,6},{8,9},{9,8},{10,11... | collective-permute-start | bytes 2543624 | tf_op jit(solution)/shard_map/ppermute | solution.py:135
  220.3 74.9 %collective-permute-start.61 = (bf16[72,2152]{1,0:T(8,128)(2,1)}, bf16[72,2152]{1,0:T(8,128)(2,1)}, u32[]{:S(2)}, u32[]{:S(2)}) collective-permute-start(bf16[72,2152]{1,0:T(8,128)(2,1)} %collective-permute-done.60), channel_id=1, source_target_pairs={{2,0},{4,2},{6,4},{8,6},{10,8},{12,10},{14,12},{16,14},{18,16},{20... | collective-permute-start | bytes 929672 | tf_op jit(solution)/shard_map/ppermute | solution.py:28
  220.8 76.0 %collective-permute-start.46 = (bf16[72,2152]{1,0:T(8,128)(2,1)}, bf16[72,2152]{1,0:T(8,128)(2,1)}, u32[]{:S(2)}, u32[]{:S(2)}) collective-permute-start(bf16[72,2152]{1,0:T(8,128)(2,1)} %collective-permute-done.45), channel_id=1, source_target_pairs={{2,0},{4,2},{6,4},{8,6},{10,8},{12,10},{14,12},{16,14},{18,16},{20... | collective-permute-start | bytes 929672 | tf_op jit(solution)/shard_map/ppermute | solution.py:28
  221.5 78.9 %collective-permute-start.54 = (bf16[72,2152]{1,0:T(8,128)(2,1)}, bf16[72,2152]{1,0:T(8,128)(2,1)}, u32[]{:S(2)}, u32[]{:S(2)}) collective-permute-start(bf16[72,2152]{1,0:T(8,128)(2,1)} %collective-permute-done.53), channel_id=1, source_target_pairs={{0,2},{2,4},{4,6},{6,8},{8,10},{10,12},{12,14},{14,16},{16,18},{18... | collective-permute-start | bytes 929672 | tf_op jit(solution)/shard_map/ppermute | solution.py:26
  222.6 70.8 %collective-permute-start.39 = (bf16[72,2152]{1,0:T(8,128)(2,1)}, bf16[72,2152]{1,0:T(8,128)(2,1)}, u32[]{:S(2)}, u32[]{:S(2)}) collective-permute-start(bf16[72,2152]{1,0:T(8,128)(2,1)} %collective-permute-done.38), channel_id=1, source_target_pairs={{0,2},{2,4},{4,6},{6,8},{8,10},{10,12},{12,14},{14,16},{16,18},{18... | collective-permute-start | bytes 929672 | tf_op jit(solution)/shard_map/ppermute | solution.py:26
  293.4 9.4 %collective-permute-start.40 = (bf16[72,2152]{1,0:T(8,128)(2,1)}, bf16[72,2152]{1,0:T(8,128)(2,1)S(1)}, u32[]{:S(2)}, u32[]{:S(2)}) collective-permute-start(bf16[72,2152]{1,0:T(8,128)(2,1)} %collective-permute-done.39), channel_id=1, source_target_pairs={{0,2},{2,4},{4,6},{6,8},{8,10},{10,12},{12,14},{14,16},{16,18},{18... | collective-permute-start | bytes 929672 | tf_op jit(solution)/shard_map/ppermute | solution.py:26
  295.2 99.8 %collective-permute-start.69 = (bf16[368,1152]{1,0:T(8,128)(2,1)}, bf16[368,1152]{1,0:T(8,128)(2,1)}, u32[]{:S(2)}, u32[]{:S(2)}) collective-permute-start(bf16[368,1152]{1,0:T(8,128)(2,1)} %get-tuple-element.80), channel_id=1, source_target_pairs={{0,1},{1,0},{2,3},{3,2},{4,5},{5,4},{6,7},{7,6},{8,9},{9,8},{10,11... | collective-permute-start | bytes 2543624 | tf_op jit(solution)/shard_map/ppermute | solution.py:135
  296.8 75.0 %collective-permute-start.62 = (bf16[72,2152]{1,0:T(8,128)(2,1)}, bf16[72,2152]{1,0:T(8,128)(2,1)}, u32[]{:S(2)}, u32[]{:S(2)}) collective-permute-start(bf16[72,2152]{1,0:T(8,128)(2,1)} %collective-permute-done.61), channel_id=1, source_target_pairs={{2,0},{4,2},{6,4},{8,6},{10,8},{12,10},{14,12},{16,14},{18,16},{20... | collective-permute-start | bytes 929672 | tf_op jit(solution)/shard_map/ppermute | solution.py:28
  300.5 64.7 %collective-permute-start.47 = (bf16[72,2152]{1,0:T(8,128)(2,1)}, bf16[72,2152]{1,0:T(8,128)(2,1)S(1)}, u32[]{:S(2)}, u32[]{:S(2)}) collective-permute-start(bf16[72,2152]{1,0:T(8,128)(2,1)} %collective-permute-done.46), channel_id=1, source_target_pairs={{2,0},{4,2},{6,4},{8,6},{10,8},{12,10},{14,12},{16,14},{18,16},{20... | collective-permute-start | bytes 929672 | tf_op jit(solution)/shard_map/ppermute | solution.py:28
  302.9 12.8 %collective-permute-start.55 = (bf16[72,2152]{1,0:T(8,128)(2,1)}, bf16[72,2152]{1,0:T(8,128)(2,1)S(1)}, u32[]{:S(2)}, u32[]{:S(2)}) collective-permute-start(bf16[72,2152]{1,0:T(8,128)(2,1)} %collective-permute-done.54), channel_id=1, source_target_pairs={{0,2},{2,4},{4,6},{6,8},{8,10},{10,12},{12,14},{14,16},{16,18},{18... | collective-permute-start | bytes 929672 | tf_op jit(solution)/shard_map/ppermute | solution.py:26
  315.6 22.7 %collective-permute-start.31 = (bf16[368,1152]{1,0:T(8,128)(2,1)S(1)}, bf16[368,1152]{1,0:T(8,128)(2,1)S(1)}, u32[]{:S(2)}, u32[]{:S(2)}) collective-permute-start(bf16[368,1152]{1,0:T(8,128)(2,1)S(1)} %convolution_convert_fusion.10), channel_id=1, source_target_pairs={{0,1},{1,0},{2,3},{3,2},{4,5},{5,4},{6,7},{7,6},{8,9},{9,8},{10,11... | collective-permute-start | bytes 2543624 | tf_op jit(solution)/shard_map/ppermute | solution.py:135
  338.3 21.5 %collective-permute-start.65 = (bf16[368,1152]{1,0:T(8,128)(2,1)S(1)}, bf16[368,1152]{1,0:T(8,128)(2,1)S(1)}, u32[]{:S(2)}, u32[]{:S(2)}) collective-permute-start(bf16[368,1152]{1,0:T(8,128)(2,1)S(1)} %convolution_convert_fusion.8), channel_id=1, source_target_pairs={{0,1},{1,0},{2,3},{3,2},{4,5},{5,4},{6,7},{7,6},{8,9},{9,8},{10,11... | collective-permute-start | bytes 2543624 | tf_op jit(solution)/shard_map/ppermute | solution.py:135
  362.9 22.1 %collective-permute-start.66 = (bf16[368,1152]{1,0:T(8,128)(2,1)S(1)}, bf16[368,1152]{1,0:T(8,128)(2,1)}, u32[]{:S(2)}, u32[]{:S(2)}) collective-permute-start(bf16[368,1152]{1,0:T(8,128)(2,1)S(1)} %get-tuple-element.96), channel_id=1, source_target_pairs={{0,1},{1,0},{2,3},{3,2},{4,5},{5,4},{6,7},{7,6},{8,9},{9,8},{10,11... | collective-permute-start | bytes 2543624 | tf_op jit(solution)/shard_map/ppermute | solution.py:135
  379.3 30.8 %collective-permute-start.32 = (bf16[368,1152]{1,0:T(8,128)(2,1)S(1)}, bf16[368,1152]{1,0:T(8,128)(2,1)S(1)}, u32[]{:S(2)}, u32[]{:S(2)}) collective-permute-start(bf16[368,1152]{1,0:T(8,128)(2,1)S(1)} %get-tuple-element.95), channel_id=1, source_target_pairs={{0,1},{1,0},{2,3},{3,2},{4,5},{5,4},{6,7},{7,6},{8,9},{9,8},{10,11... | collective-permute-start | bytes 2543624 | tf_op jit(solution)/shard_map/ppermute | solution.py:135
  408.1 71.8 %collective-permute-start.71 = (bf16[368,1152]{1,0:T(8,128)(2,1)}, bf16[368,1152]{1,0:T(8,128)(2,1)}, u32[]{:S(2)}, u32[]{:S(2)}) collective-permute-start(bf16[368,1152]{1,0:T(8,128)(2,1)} %convolution_convert_fusion.5), channel_id=1, source_target_pairs={{0,1},{1,0},{2,3},{3,2},{4,5},{5,4},{6,7},{7,6},{8,9},{9,8},{10,11... | collective-permute-start | bytes 2543624 | tf_op jit(solution)/shard_map/ppermute | solution.py:135
  435.3 51.4 %collective-permute-start.70 = (bf16[368,1152]{1,0:T(8,128)(2,1)}, bf16[368,1152]{1,0:T(8,128)(2,1)}, u32[]{:S(2)}, u32[]{:S(2)}) collective-permute-start(bf16[368,1152]{1,0:T(8,128)(2,1)} %convolution_convert_fusion.6), channel_id=1, source_target_pairs={{0,1},{1,0},{2,3},{3,2},{4,5},{5,4},{6,7},{7,6},{8,9},{9,8},{10,11... | collective-permute-start | bytes 2543624 | tf_op jit(solution)/shard_map/ppermute | solution.py:135
  499.6 21.9 %collective-permute-start.74 = (bf16[368,1152]{1,0:T(8,128)(2,1)S(1)}, bf16[368,1152]{1,0:T(8,128)(2,1)S(1)}, u32[]{:S(2)}, u32[]{:S(2)}) collective-permute-start(bf16[368,1152]{1,0:T(8,128)(2,1)S(1)} %convert_element_type.297), channel_id=1, source_target_pairs={{0,1},{1,0},{2,3},{3,2},{4,5},{5,4},{6,7},{7,6},{8,9},{9,8},{10,11... | collective-permute-start | bytes 2543624 | tf_op jit(solution)/shard_map/ppermute | solution.py:135
  501.7 61.6 %collective-permute-start.72 = (bf16[368,1152]{1,0:T(8,128)(2,1)S(1)}, bf16[368,1152]{1,0:T(8,128)(2,1)S(1)}, u32[]{:S(2)}, u32[]{:S(2)}) collective-permute-start(bf16[368,1152]{1,0:T(8,128)(2,1)S(1)} %convert_element_type.281), channel_id=1, source_target_pairs={{0,1},{1,0},{2,3},{3,2},{4,5},{5,4},{6,7},{7,6},{8,9},{9,8},{10,11... | collective-permute-start | bytes 2543624 | tf_op jit(solution)/shard_map/ppermute | solution.py:135
  593.0 177.2 %reduce-scatter.11.cloned.1.call-start = ((), (), s32[]{:S(2)}) async-start(), calls=%async_computation.4 | async-start | bytes 4386816 | tf_op jit(solution)/shard_map/reduce_scatter | solution.py:159
  629.0 177.0 %reduce-scatter.17.cloned.1.call-start = ((), (), s32[]{:S(2)}) async-start(), calls=%async_computation.7 | async-start | bytes 5326848
  629.8 257.6 %reduce-scatter.15.cloned.1.call-start = ((), (), s32[]{:S(2)}) async-start(), calls=%async_computation.6 | async-start | bytes 5326848
  638.1 22.1 %collective-permute-start.67 = (bf16[368,1152]{1,0:T(8,128)(2,1)}, bf16[368,1152]{1,0:T(8,128)(2,1)}, u32[]{:S(2)}, u32[]{:S(2)}) collective-permute-start(bf16[368,1152]{1,0:T(8,128)(2,1)} %convolution_convert_fusion.7), channel_id=1, source_target_pairs={{0,1},{1,0},{2,3},{3,2},{4,5},{5,4},{6,7},{7,6},{8,9},{9,8},{10,11... | collective-permute-start | bytes 2543624 | tf_op jit(solution)/shard_map/ppermute | solution.py:135
  645.8 26.2 %collective-permute-start.63 = (bf16[368,1152]{1,0:T(8,128)(2,1)}, bf16[368,1152]{1,0:T(8,128)(2,1)}, u32[]{:S(2)}, u32[]{:S(2)}) collective-permute-start(bf16[368,1152]{1,0:T(8,128)(2,1)} %convolution_convert_fusion.9), channel_id=1, source_target_pairs={{0,1},{1,0},{2,3},{3,2},{4,5},{5,4},{6,7},{7,6},{8,9},{9,8},{10,11... | collective-permute-start | bytes 2543624 | tf_op jit(solution)/shard_map/ppermute | solution.py:135
  685.0 28.6 %collective-permute-start.75 = (bf16[368,1152]{1,0:T(8,128)(2,1)S(1)}, bf16[368,1152]{1,0:T(8,128)(2,1)S(1)}, u32[]{:S(2)}, u32[]{:S(2)}) collective-permute-start(bf16[368,1152]{1,0:T(8,128)(2,1)S(1)} %convolution_convert_fusion.3), channel_id=1, source_target_pairs={{0,1},{1,0},{2,3},{3,2},{4,5},{5,4},{6,7},{7,6},{8,9},{9,8},{10,11... | collective-permute-start | bytes 2543624 | tf_op jit(solution)/shard_map/ppermute | solution.py:135
  688.0 29.5 %collective-permute-start.73 = (bf16[368,1152]{1,0:T(8,128)(2,1)S(1)}, bf16[368,1152]{1,0:T(8,128)(2,1)S(1)}, u32[]{:S(2)}, u32[]{:S(2)}) collective-permute-start(bf16[368,1152]{1,0:T(8,128)(2,1)S(1)} %convolution_convert_fusion.4), channel_id=1, source_target_pairs={{0,1},{1,0},{2,3},{3,2},{4,5},{5,4},{6,7},{7,6},{8,9},{9,8},{10,11... | collective-permute-start | bytes 2543624 | tf_op jit(solution)/shard_map/ppermute | solution.py:135
  (129 other events, 1566.8 us)
Sparse Core Ops, SparseCore 0:
  593.1 56.3 reduce-scatter.12
  653.4 70.9 reduce-scatter.10
  728.4 77.5 reduce-scatter.16
  810.4 76.9 reduce-scatter.14
